TPU v7x, 512 devices: a whole 4x8x8 slice. The times are simulated.
512 devices in a mesh: dp: 32 (over x_hi, y, core), fsdp: 16 (over z, x_lo).
Axes of the slice: x: 4 (x_hi: 2, x_lo: 2; x = x_hi * 2 + x_lo), y: 8, z: 8, core: 2. Of those that a mesh axis runs over, the one named last changes fastest.
Arguments:
- latents: bfloat16 [1024, 96, 1024], P(('dp', 'fsdp')), may hold values from -6 to 6
- targets: bfloat16 [1024, 96, 1024], P(('dp', 'fsdp')), may hold values from -6 to 6
- rewards: float32 [1024], P(('dp', 'fsdp')), may hold values from 0.2 to 5
- time_steps: int32 [1024], P(('dp', 'fsdp')), may hold values from 0 to 999
- time_table: float32 [1000, 96], replicated, may hold values from -6 to 6
- norm_gain: float32 [96], replicated, may hold values from 0.5 to 1.5
- norm_bias: float32 [96], replicated, may hold values from -3 to 3
- expert_weights: bfloat16 [8, 96, 2592], P(None, 'fsdp'), may hold values from -0.125 to 0.125
- lane_experts: int32 [32, 2], P('dp'), may hold values from 0 to 7, all different within a row
- lane_counts: int32 [32, 2], P('dp'), may hold values from 1 to 31, as said below
Outputs:
- grad_weight: float32 [8, 96, 2592], P(None, 'fsdp')
- grad_input: bfloat16 [1024, 96, 1024], P(('dp', 'fsdp'))
Inputs may be any that keep to these rules, and one draw needn't show every extreme that they name: `lane_experts`: the two experts of a lane differ, and every expert belongs to some lane. `lane_counts`: both counts of a lane are at least 1 and add up to at most 32; some lane is full in every draw. A lane's slots hold its first expert's samples, then its second's, then empty slots.
All inputs are finite; a program needn't handle non-finite values.
Results may differ from a plain program's by a relative error of at most 0.015.
Values may be sent and summed in bfloat16 or wider, within the bound.
A program may use at most 64 MiB of HBM per device.

v0:
```python
import jax
import jax.numpy as jnp
from jax import lax
from jax.sharding import PartitionSpec as P

GROUPS = 32
SIDE = 16
DEPTH = 4


EPSILON = 1e-05


def tap_list():
    result = []
    for step_x in (-1, 0, 1):
        for step_y in (-1, 0, 1):
            for step_z in (-1, 0, 1):
                result.append((step_x, step_y, step_z))
    return result


def shift_cells(values, step_x, step_y, step_z):
    plane = SIDE * SIDE
    total = DEPTH * plane
    position = jnp.arange(total, dtype=jnp.int32)
    depth_at = position // plane
    row_at = position // SIDE % SIDE
    column_at = position % SIDE
    inside = (
        (depth_at + step_x >= 0)
        & (depth_at + step_x < DEPTH)
        & (row_at + step_y >= 0)
        & (row_at + step_y < SIDE)
        & (column_at + step_z >= 0)
        & (column_at + step_z < SIDE)
    )
    offset = step_x * plane + step_y * SIDE + step_z
    reach = plane + SIDE + 1
    widths = [(0, 0)] * (values.ndim - 1) + [(reach, reach)]
    padded = jnp.pad(values, widths)
    moved_cells = lax.slice_in_dim(
        padded, reach + offset, reach + offset + total, axis=values.ndim - 1
    )
    return jnp.where(inside, moved_cells, jnp.zeros_like(moved_cells))


def unfold_taps(activ_rows):
    pieces = []
    for offset in tap_list():
        pieces.append(shift_cells(activ_rows, offset[0], offset[1], offset[2]))
    return jnp.concatenate(pieces, axis=0)


def norm_act(field, norm_gain, norm_bias):
    lead = field.shape[:-2]
    channels = field.shape[-2]
    grouped = field.reshape(lead + (GROUPS, channels // GROUPS * field.shape[-1]))
    centre = jnp.mean(grouped, axis=-1, keepdims=True)
    spread = jnp.mean(jnp.square(grouped - centre), axis=-1, keepdims=True)
    normed = ((grouped - centre) * lax.rsqrt(spread + EPSILON)).reshape(field.shape)
    return jax.nn.silu(normed * norm_gain[:, None] + norm_bias[:, None])


def local(
    latents,
    targets,
    rewards,
    time_steps,
    time_table,
    norm_gain,
    norm_bias,
    expert_weights,
    lane_experts,
    lane_counts,
):
    slots = latents.shape[0]
    channels = latents.shape[1]
    experts_all = expert_weights.shape[0]
    offsets = tap_list()
    lane_pair = lane_experts[0]
    counts = lane_counts[0]
    place = lax.axis_index("fsdp") * slots + jnp.arange(slots, dtype=jnp.int32)
    in_first = place < counts[0]
    in_second = (place >= counts[0]) & (place < counts[0] + counts[1])
    member = jnp.stack([in_first, in_second], axis=1).astype(jnp.float32)
    which = jnp.where(in_second, 1, 0).astype(jnp.int32)
    slot_weight = rewards * jnp.sum(member, axis=1)
    pick = (lane_pair[:, None] == jnp.arange(experts_all, dtype=jnp.int32)[None, :]).astype(
        jnp.float32
    )
    lane_shards = jnp.einsum(
        "je,erk->jrk", pick.astype(jnp.bfloat16), expert_weights, preferred_element_type=jnp.float32
    ).astype(jnp.bfloat16)
    table_rows = time_table.shape[0]
    one_hot = (time_steps[:, None] == jnp.arange(table_rows, dtype=jnp.int32)[None, :]).astype(
        jnp.float32
    )
    embedded = jnp.dot(
        one_hot, time_table, precision=lax.Precision.HIGHEST, preferred_element_type=jnp.float32
    )
    starts = latents.astype(jnp.float32) + embedded[:, :, None]
    activ, back_fn = jax.vjp(lambda field: norm_act(field, norm_gain, norm_bias), starts)
    activ_b = activ.astype(jnp.bfloat16)
    columns = [unfold_taps(activ_b[slot_index]) for slot_index in range(slots)]
    holder = {}
    piece = lax.all_gather(lane_shards, "fsdp", axis=1, tiled=True)
    outputs = []
    for slot_index in range(slots):
        chosen = lax.dynamic_index_in_dim(piece, which[slot_index], 0, keepdims=False)
        outputs.append(jnp.dot(chosen, columns[slot_index], preferred_element_type=jnp.float32))
    mixed = jnp.stack(outputs, axis=0)
    upstream = slot_weight[:, None, None] * (
        latents.astype(jnp.float32) + mixed - targets.astype(jnp.float32)
    )
    upstream_b = upstream.astype(jnp.bfloat16)
    holder["upstream"] = upstream_b
    cells = latents.shape[2]
    pieces = []
    for weight_slot_index in range(slots):
        weight_rows_grad = upstream_b[weight_slot_index]
        pieces.append(
            lax.dot_general(
                weight_rows_grad,
                columns[weight_slot_index],
                (((1,), (1,)), ((), ())),
                preferred_element_type=jnp.float32,
            )
        )
    stacked = jnp.stack(pieces, axis=0) / cells
    share = lax.psum_scatter(
        jnp.einsum("sj,srk->rjk", member, stacked, precision=lax.Precision.HIGHEST).astype(
            jnp.bfloat16
        ),
        "fsdp",
        scatter_dimension=0,
        tiled=True,
    ).astype(jnp.float32)
    piece = lax.all_gather(lane_shards, "fsdp", axis=1, tiled=True)
    add_upstream_b = holder["upstream"]
    updates = []
    for slot_index in range(slots):
        chosen = lax.dynamic_index_in_dim(piece, which[slot_index], 0, keepdims=False)
        rows_grad = add_upstream_b[slot_index]
        total = jnp.zeros((channels, rows_grad.shape[1]), jnp.float32)
        for plane_index in range(3):
            block = chosen[:, plane_index * 9 * channels : (plane_index + 1) * 9 * channels]
            products = lax.dot_general(
                block, rows_grad, (((0,), (0,)), ((), ())), preferred_element_type=jnp.float32
            )
            for tap_inner in range(9):
                offset = offsets[plane_index * 9 + tap_inner]
                part_rows = products[tap_inner * channels : (tap_inner + 1) * channels]
                total = total + shift_cells(part_rows, -offset[0], -offset[1], -offset[2])
        updates.append(total)
    grad_act = jnp.stack(updates, axis=0)
    table = jnp.einsum("je,rjk->erk", pick, share, precision=lax.Precision.HIGHEST)
    grad_weight = lax.psum(table.astype(jnp.bfloat16), "dp").astype(jnp.float32)
    grad_start = back_fn(grad_act)[0]
    grad_input = (upstream + grad_start).astype(jnp.bfloat16)
    return (grad_weight, grad_input)


def solution(mesh):
    placed = (
        P(("dp", "fsdp"), None, None),
        P(("dp", "fsdp"), None, None),
        P(("dp", "fsdp")),
        P(("dp", "fsdp")),
        P(),
        P(),
        P(),
        P(None, "fsdp", None),
        P("dp", None),
        P("dp", None),
    )
    return jax.shard_map(
        local,
        mesh=mesh,
        in_specs=placed,
        out_specs=(P(None, "fsdp", None), P(("dp", "fsdp"), None, None)),
        check_vma=False,
    )
```

profile of v0, /device:TPU:1, one launch (start us, length us, event | category | flops | bytes accessed | tf_op | source)
XLA Modules:
  0.0 511.6 jit_solution(13347033625417734909)
XLA Ops:
  7.4 1.3 fusion.296
  10.1 0.6 and_select_fusion
  10.7 0.7 fusion.295
  14.1 0.7 compare_and_fusion
  14.7 0.9 fusion.246
  15.7 1.2 fusion.3
  17.3 1.3 fusion.13
  19.0 1.5 multiply_convert_fusion
  20.5 1.2 convolution_convert_fusion.2
  21.8 40.3 %all_gather.4 = bf16[2,96,2592]{2,0,1:T(2,128)(2,1)S(1)} all-gather(bf16[2,6,2592]{2,0,1:T(2,128)(2,1)S(1)} %convolution_convert_fusion.2), channel_id=1, replica_groups=mesh['dp'=32,'fsdp'=16] {'fsdp'}, dimensions={1}, use_global_device_ids=true | all-gather | bytes 1057536 | tf_op jit(solution)/shard_map/all_gather | solution.py:107
  63.4 2.1 constant_dynamic-slice_fusion.1
  70.1 1.0 convolution_bitcast_fusion.2
  71.2 1.0 convolution_bitcast_fusion.3
  72.5 1.8 convolution_bitcast_fusion
  74.3 1.8 convolution_bitcast_fusion.1
  76.2 6.7 %fusion = bf16[96,2,2592]{2,1,0:T(2,128)(2,1)} fusion(f32[2,96,2592]{2,1,0:T(8,128)S(1)} %maximum_multiply_fusion, pred[2,1]{0,1:T(4,128)(4,1)S(1)} %get-tuple-element.119, pred[2,1]{0,1:T(4,128)(4,1)S(1)} %get-tuple-element.120), kind=kOutput, calls=%fused_computation.1 | convolution fusion | flops 12441604 | bytes 2985988 | tf_op jit(solution)/shard_map/sj,srk->rjk/dot_general | solution.py:132
  83.0 0.7 fusion.232
  83.7 0.7 fusion.234
  84.4 0.6 fusion.236
  85.1 0.7 fusion.238
  85.8 0.7 fusion.240
  86.5 0.6 fusion.242
  87.2 0.5 fusion.294
  89.8 2.2 fusion.124
  92.1 2.2 fusion.71
  94.4 0.7 multiply_reduce_fusion
  96.4 1.3 dynamic-slice
  98.3 123.5 %all-reduce.60.cloned.1.call-done = bf16[96,2,2592]{2,1,0:T(2,128)(2,1)} async-done(((bf16[96,2,2592]{2,1,0:T(2,128)(2,1)}), bf16[96,2,2592]{2,1,0:T(2,128)(2,1)}) %all-reduce.60.cloned.1.call-update) | async-done | bytes 995344
  221.8 1.9 convolution_convert_fusion.1
  223.7 1.1 fusion.12
  224.8 278.1 %all-reduce.58.cloned.1.call-done = bf16[8,6,2592]{2,0,1:T(8,128)(2,1)} async-done(((bf16[8,6,2592]{2,0,1:T(8,128)(2,1)}), bf16[8,6,2592]{2,0,1:T(8,128)(2,1)}) %all-reduce.58.cloned.1.call-update) | async-done | bytes 248848 | tf_op jit(solution)/shard_map/psum | solution.py:158
  503.0 1.8 convert_element_type.163
  (95 shorter events, 9.2 us)
Async XLA Ops:
  7.2 7.6 %copy-start = (f32[1000,96]{0,1:T(8,128)S(1)}, f32[1000,96]{0,1:T(8,128)}, u32[]{:S(2)}) copy-start(f32[1000,96]{0,1:T(8,128)} %param.14) | copy-start | bytes 1152004
  7.2 214.6 %all-reduce.60.cloned.1.call-start = ((), (), s32[]{:S(2)}) async-start(), calls=%async_computation.1 | async-start | bytes 2064384
  70.1 2.1 copy-start.7
  70.1 2.1 copy-start.2
  70.1 2.1 copy-start.3
  82.9 420.0 %all-reduce.58.cloned.1.call-start = ((), (), s32[]{:S(2)}) async-start(), calls=%async_computation | async-start | bytes 516096 | tf_op jit(solution)/shard_map/psum | solution.py:158
  92.0 2.3 copy-start.4
  92.1 2.3 copy-start.5
  92.1 129.8 %copy-start.6 = (s32[1,2]{1,0:T(1,128)S(1)}, s32[1,2]{1,0:T(1,128)}, u32[]{:S(2)}) copy-start(s32[1,2]{1,0:T(1,128)} %param.18) | copy-start | bytes 28
  92.1 412.7 %copy-start.1 = (f32[1000,96]{0,1:T(8,128)S(1)}, f32[1000,96]{0,1:T(8,128)}, u32[]{:S(2)}) copy-start(f32[1000,96]{0,1:T(8,128)} %param.14) | copy-start | bytes 1152004
Sparse Core Ops, SparseCore 0:
  83.1 138.7 all-reduce.59
  225.6 277.3 all-reduce.57
where the time goes:
time: 512 us
  waiting for transfers between devices  402 us (79%)
  blocking collectives  40.3 us (8%)
  matrix products  20.6 us (4%)
  between operations  20.6 us (4%)
  other arithmetic  18.9 us (4%)
  local copies, waits for them, and re-layouts  9.45 us (2%)
    psum x1, waiting for transfers between devices, local(): grad_weight = lax.psum(table.astype(jnp.bfloat16), 'dp').astype(jnp.float32)  278 us
    unnamed x3, waiting for transfers between devices  124 us
    all_gather x1, blocking collectives, local(): piece = lax.all_gather(lane_shards, 'fsdp', axis=1, tiled=True)  40.3 us
  transfers between devices with their start and end apart: 2, of which 2 were waited for; matrix products, arithmetic and copies ran while one was open for 3% of the time, Pallas kernels for 0%

commit v1 on v0

--- a/solution.py
+++ b/solution.py
@@ -1,6 +1,8 @@
 import jax
 import jax.numpy as jnp
 from jax import lax
+from jax.experimental import pallas as pl
+from jax.experimental.pallas import tpu as pltpu
 from jax.sharding import PartitionSpec as P
 
 GROUPS = 32
@@ -9,6 +11,250 @@
 
 
 EPSILON = 1e-05
+
+MESH = pl.DeviceIdType.MESH
+ROWS = 16
+WIDE = 2688
+TILES = 21
+VMEM = pl.BlockSpec(memory_space=pltpu.VMEM)
+
+
+def rcopy(src, dst, sems, at, device_id):
+    return pltpu.make_async_remote_copy(
+        src_ref=src,
+        dst_ref=dst,
+        send_sem=sems[0].at[at],
+        recv_sem=sems[1].at[at],
+        device_id=device_id,
+        device_id_type=MESH,
+    )
+
+
+def ring_place():
+    f = lax.axis_index("fsdp")
+    z = f // 2
+    x = f % 2
+    nbr = z * 2 + 1 - x
+    up = lax.rem(z + 1, 8) * 2 + x
+    down = lax.rem(z + 7, 8) * 2 + x
+    return f, z, x, nbr, up, down
+
+
+def gather_kernel(shard_ref, out_ref, send_sem, recv_sem):
+    f, z, x, nbr, up, down = ring_place()
+    sems = (send_sem, recv_sem)
+    barrier = pltpu.get_barrier_semaphore()
+    for other in (nbr, up, down):
+        pl.semaphore_signal(barrier, inc=1, device_id={"fsdp": other}, device_id_type=MESH)
+    pl.semaphore_wait(barrier, 3)
+    out_ref[f] = shard_ref[...]
+    hops = {(0, 0): 4, (0, 1): 3, (1, 0): 3, (1, 1): 4}
+    base = {}
+    count = 1
+    for key, n in hops.items():
+        base[key] = count
+        count += n
+
+    def make(key, h):
+        col, direction = key
+        zz = lax.rem(z + 8 - h, 8) if direction == 0 else lax.rem(z + h, 8)
+        item = zz * 2 + (x if col == 0 else 1 - x)
+        return rcopy(
+            out_ref.at[item], out_ref.at[item], sems, base[key] + h,
+            {"fsdp": up if direction == 0 else down},
+        )
+
+    copies = {}
+    swap = rcopy(shard_ref, out_ref.at[f], sems, 0, {"fsdp": nbr})
+    swap.start()
+    for key in ((0, 0), (0, 1)):
+        copies[key] = [make(key, 0)]
+        copies[key][0].start()
+    swap.wait_recv()
+    for key in ((1, 0), (1, 1)):
+        copies[key] = [make(key, 0)]
+        copies[key][0].start()
+    for h in range(1, 5):
+        for key, n in hops.items():
+            if h <= n:
+                copies[key][h - 1].wait_recv()
+            if h < n:
+                copies[key].append(make(key, h))
+                copies[key][h].start()
+    swap.wait_send()
+    for key in hops:
+        for copy in copies[key]:
+            copy.wait_send()
+
+
+def gather(shard):
+    return pl.pallas_call(
+        gather_kernel,
+        out_shape=jax.ShapeDtypeStruct((16, ROWS, WIDE), jnp.bfloat16),
+        in_specs=[VMEM],
+        out_specs=VMEM,
+        scratch_shapes=[pltpu.SemaphoreType.DMA((15,)), pltpu.SemaphoreType.DMA((15,))],
+        compiler_params=pltpu.CompilerParams(
+            collective_id=0, has_side_effects=True, vmem_limit_bytes=40 * 2**20
+        ),
+    )(shard)
+
+
+def reduce_kernel(
+    part_ref, place_ref, out_ref, held, stage, total, swap_out, swap_in, table, core_in, half,
+    chunk_in, full, ring_s, ring_r, dp_s, dp_r,
+):
+    f, z, x, nbr, up, down = ring_place()
+    ring = (ring_s, ring_r)
+    lanes = (dp_s, dp_r)
+    d = lax.axis_index("dp")
+    core = d % 2
+    chip = d // 2
+    twin = chip * 2 + 1 - core
+    peers = [lax.rem(chip + i, 16) for i in range(1, 16)]
+    barrier = pltpu.get_barrier_semaphore()
+    for other in (nbr, up, down):
+        pl.semaphore_signal(barrier, inc=1, device_id={"fsdp": other}, device_id_type=MESH)
+    pl.semaphore_signal(barrier, inc=1, device_id={"dp": twin}, device_id_type=MESH)
+    for peer in peers:
+        pl.semaphore_signal(
+            barrier, inc=1, device_id={"dp": peer * 2 + core}, device_id_type=MESH
+        )
+    pl.semaphore_wait(barrier, 19)
+
+    f32 = jnp.float32
+    hops = {(0, 0): 4, (0, 1): 3, (1, 0): 3, (1, 1): 4}
+    base = {}
+    count = 0
+    for key, n in hops.items():
+        base[key] = count
+        count += n
+    copies = {}
+    for h in range(4):
+        for key, n in hops.items():
+            if h >= n:
+                continue
+            col, direction = key
+            away = n - h
+            zz = lax.rem(z + away, 8) if direction == 0 else lax.rem(z + 8 - away, 8)
+            at = base[key] + h
+            if h == 0:
+                src = part_ref.at[zz * 2 + col]
+                copies[key] = []
+            else:
+                copies[key][h - 1].wait_recv()
+                stage[at] = (
+                    held[at - 1].astype(f32) + part_ref[zz * 2 + col].astype(f32)
+                ).astype(jnp.bfloat16)
+                src = stage.at[at]
+            copy = rcopy(src, held.at[at], ring, at, {"fsdp": up if direction == 0 else down})
+            copy.start()
+            copies[key].append(copy)
+    for col in (0, 1):
+        for direction in (0, 1):
+            key = (col, direction)
+            copies[key][-1].wait_recv()
+        value = (
+            part_ref[z * 2 + col].astype(f32)
+            + held[base[(col, 0)] + hops[(col, 0)] - 1].astype(f32)
+            + held[base[(col, 1)] + hops[(col, 1)] - 1].astype(f32)
+        )
+        total[col] = value
+        swap_out[col] = value.astype(jnp.bfloat16)
+    swap = rcopy(swap_out.at[1 - x], swap_in, ring, 14, {"fsdp": nbr})
+    swap.start()
+    swap.wait_recv()
+    lane = (total[x] + swap_in[...].astype(f32)).astype(jnp.bfloat16)
+    spread = jnp.dot(place_ref[...], lane, preferred_element_type=f32).astype(jnp.bfloat16)
+    for row in range(3):
+        for tile in range(TILES):
+            table[row * TILES + tile] = spread[
+                row * ROWS : (row + 1) * ROWS, tile * 128 : (tile + 1) * 128
+            ]
+    table[63] = jnp.zeros((ROWS, 128), jnp.bfloat16)
+
+    mine = core * 32
+    pair = rcopy(table.at[pl.ds(32 - mine, 32)], core_in, lanes, 30, {"dp": twin})
+    pair.start()
+    pair.wait_recv()
+    half[...] = (table[pl.ds(mine, 32)].astype(f32) + core_in[...].astype(f32)).astype(
+        jnp.bfloat16
+    )
+    scatters = []
+    for i, peer in enumerate(peers):
+        copy = rcopy(
+            half.at[pl.ds(peer * 2, 2)], chunk_in.at[i], lanes, i, {"dp": peer * 2 + core}
+        )
+        copy.start()
+        scatters.append(copy)
+    acc = half[pl.ds(chip * 2, 2)].astype(f32)
+    for i, copy in enumerate(scatters):
+        copy.wait_recv()
+        acc = acc + chunk_in[i].astype(f32)
+    own = pl.ds(mine + chip * 2, 2)
+    full[own] = acc.astype(jnp.bfloat16)
+    gathers = []
+    for i, peer in enumerate(peers):
+        copy = rcopy(full.at[own], full.at[own], lanes, 15 + i, {"dp": peer * 2 + core})
+        copy.start()
+        gathers.append(copy)
+    for copy in gathers:
+        copy.wait_recv()
+    both = pl.ds(mine, 32)
+    last = rcopy(full.at[both], full.at[both], lanes, 31, {"dp": twin})
+    last.start()
+    last.wait_recv()
+    for tile in range(TILES):
+        block = jnp.concatenate(
+            [full[row * TILES + tile].astype(f32) for row in range(3)], axis=0
+        )
+        wide = min(128, 2592 - tile * 128)
+        for expert in range(8):
+            out_ref[expert, :, tile * 128 : tile * 128 + wide] = block[
+                expert * 6 : expert * 6 + 6, :wide
+            ]
+    for key in hops:
+        for copy in copies[key]:
+            copy.wait_send()
+    swap.wait_send()
+    pair.wait_send()
+    last.wait_send()
+    for copy in scatters + gathers:
+        copy.wait_send()
+
+
+def reduce_all(part, place):
+    bf16 = jnp.bfloat16
+    return pl.pallas_call(
+        reduce_kernel,
+        out_shape=jax.ShapeDtypeStruct((8, 6, 2592), jnp.float32),
+        in_specs=[VMEM, VMEM],
+        out_specs=VMEM,
+        scratch_shapes=[
+            pltpu.VMEM((14, ROWS, WIDE), bf16),
+            pltpu.VMEM((14, ROWS, WIDE), bf16),
+            pltpu.VMEM((2, ROWS, WIDE), jnp.float32),
+            pltpu.VMEM((2, ROWS, WIDE), bf16),
+            pltpu.VMEM((ROWS, WIDE), bf16),
+            pltpu.VMEM((64, ROWS, 128), bf16),
+            pltpu.VMEM((32, ROWS, 128), bf16),
+            pltpu.VMEM((32, ROWS, 128), bf16),
+            pltpu.VMEM((15, 2, ROWS, 128), bf16),
+            pltpu.VMEM((64, ROWS, 128), bf16),
+            pltpu.SemaphoreType.DMA((15,)),
+            pltpu.SemaphoreType.DMA((15,)),
+            pltpu.SemaphoreType.DMA((32,)),
+            pltpu.SemaphoreType.DMA((32,)),
+        ],
+        compiler_params=pltpu.CompilerParams(
+            collective_id=1, has_side_effects=True, vmem_limit_bytes=40 * 2**20
+        ),
+    )(part, place)
+
+
+def place_matrix(pick):
+    body = jnp.einsum("je,rq->erjq", pick, jnp.eye(6, dtype=jnp.float32)).reshape(48, 12)
+    return jnp.pad(body, ((0, 0), (0, 4))).astype(jnp.bfloat16)
 
 
 def tap_list():
@@ -104,7 +350,8 @@
     activ_b = activ.astype(jnp.bfloat16)
     columns = [unfold_taps(activ_b[slot_index]) for slot_index in range(slots)]
     holder = {}
-    piece = lax.all_gather(lane_shards, "fsdp", axis=1, tiled=True)
+    shard = jnp.pad(lane_shards.reshape(12, -1), ((0, 4), (0, WIDE - 2592)))
+    piece = gather(shard)[:, :12, :2592].reshape(16, 2, 6, 2592).swapaxes(0, 1).reshape(2, 96, 2592)
     outputs = []
     for slot_index in range(slots):
         chosen = lax.dynamic_index_in_dim(piece, which[slot_index], 0, keepdims=False)
@@ -128,15 +375,12 @@
             )
         )
     stacked = jnp.stack(pieces, axis=0) / cells
-    share = lax.psum_scatter(
-        jnp.einsum("sj,srk->rjk", member, stacked, precision=lax.Precision.HIGHEST).astype(
-            jnp.bfloat16
-        ),
-        "fsdp",
-        scatter_dimension=0,
-        tiled=True,
-    ).astype(jnp.float32)
-    piece = lax.all_gather(lane_shards, "fsdp", axis=1, tiled=True)
+    sums = jnp.einsum("sj,srk->rjk", member, stacked, precision=lax.Precision.HIGHEST).astype(
+        jnp.bfloat16
+    )
+    part = sums.reshape(16, 6, 2, 2592).swapaxes(1, 2).reshape(16, 12, 2592)
+    part = jnp.pad(part, ((0, 0), (0, 4), (0, WIDE - 2592)))
+    grad_weight = reduce_all(part, place_matrix(pick))
     add_upstream_b = holder["upstream"]
     updates = []
     for slot_index in range(slots):
@@ -154,8 +398,6 @@
                 total = total + shift_cells(part_rows, -offset[0], -offset[1], -offset[2])
         updates.append(total)
     grad_act = jnp.stack(updates, axis=0)
-    table = jnp.einsum("je,rjk->erk", pick, share, precision=lax.Precision.HIGHEST)
-    grad_weight = lax.psum(table.astype(jnp.bfloat16), "dp").astype(jnp.float32)
     grad_start = back_fn(grad_act)[0]
     grad_input = (upstream + grad_start).astype(jnp.bfloat16)
     return (grad_weight, grad_input)

time: 512 us -> 137 us (0.27)
  waiting for transfers between devices: 402 us -> 0 us
  Pallas kernels: 0 us -> 77.4 us
  blocking collectives: 40.3 us -> 0 us
  between operations: 20.6 us -> 6.66 us
  local copies, waits for them, and re-layouts: 9.45 us -> 15.7 us
    psum x1 -> x0, waiting for transfers between devices: 278 us -> none  [local(): grad_weight = lax.psum(table.astype(jnp.bfloat16), 'dp').astype(jnp.float32)]
    unnamed x3 -> x0, waiting for transfers between devices: 124 us -> none
    pallas_call x0 -> x2, Pallas kernels: none -> 77.4 us  [the longest x1 50.4 us: reduce_all(): pl.pallas_call(reduce_kernel, out_shape=jax.ShapeDtypeStruct((8, 6, 2592)...]
    all_gather x1 -> x0, blocking collectives: 40.3 us -> none  [local(): piece = lax.all_gather(lane_shards, 'fsdp', axis=1, tiled=True)]
    unnamed x17 -> x44, local copies, waits for them, and re-layouts: 1.33 us -> 6.87 us
  transfers between devices with their start and end apart: 2 -> 0, of which waited for: 2 -> 0; matrix products, arithmetic and copies ran while one was open for 3% -> 0% of each run, Pallas kernels for 0% -> 0%
where the time goes in v1:
time: 137 us
  Pallas kernels  77.4 us (56%)
  matrix products  19.6 us (14%)
  other arithmetic  17.3 us (13%)
  local copies, waits for them, and re-layouts  15.7 us (11%)
  between operations  6.66 us (5%)
    pallas_call x1, Pallas kernels, reduce_all(): pl.pallas_call(reduce_kernel, out_shape=jax.ShapeDtypeStruct((8, 6, 2592)...  50.4 us
    pallas_call x1, Pallas kernels, gather(): pl.pallas_call(gather_kernel, out_shape=jax.ShapeDtypeStruct((16, ROWS, W...  27.1 us
    unnamed x44, local copies, waits for them, and re-layouts  6.87 us
    dot_general x1, matrix products, local(): jnp.einsum('sj,srk->rjk', member, stacked, precision=lax.Precision.HIGHEST)  5.76 us
    dot_general x2, matrix products, local(): jnp.dot(chosen, columns[slot_index], preferred_element_type=jnp.float32)  4.71 us
    another operation x2, other arithmetic, local(): grad_act = jnp.stack(updates, axis=0)  4.48 us
    dot_general x6, matrix products, local(): lax.dot_general(block, rows_grad, (((0,), (0,)), ((), ())), preferred_ele...  4.18 us
    unnamed x28, other arithmetic  4.06 us

profile of v1, /device:TPU:1, one launch (start us, length us, event | category | flops | bytes accessed | tf_op | source)
XLA Modules:
  0.0 136.7 jit_solution(7378306137729510224)
XLA Ops:
  0.6 1.0 copy-done
  1.6 0.9 fusion.245
  2.6 1.2 fusion.2
  4.2 1.3 fusion.12
  5.9 1.5 %multiply_convert_fusion = bf16[2,96,1024]{2,1,0:T(8,128)(2,1)S(1)} fusion(bf16[2,96,1024]{2,1,0:T(8,128)(2,1)} %param.10, f32[96]{0:T(128)} %param.16, f32[96]{0:T(128)} %param.15, f32[2,96]{1,0:T(2,128)S(1)} %mul.109, f32[2,96]{1,0:T(2,128)S(1)} %sub.897, f32[2,96]{1,0:T(2,128)S(1)} %fusion.245), kind=kLoop, calls=%fused_computation.84 | loop fusion | flops 2162688 | bytes 789504 | tf_op jit(solution)/shard_map/convert_element_type | solution.py:350
  12.1 2.4 %copy-done.2 = bf16[2592,1024]{1,0:T(8,128)(2,1)} copy-done((bf16[2592,1024]{1,0:T(8,128)(2,1)}, bf16[2592,1024]{1,0:T(8,128)(2,1)S(1)}, u32[]{:S(2)}) %copy-start.2) | copy-done | bytes 5308440
  14.5 2.4 %copy-done.3 = bf16[2592,1024]{1,0:T(8,128)(2,1)} copy-done((bf16[2592,1024]{1,0:T(8,128)(2,1)}, bf16[2592,1024]{1,0:T(8,128)(2,1)S(1)}, u32[]{:S(2)}) %copy-start.3) | copy-done | bytes 5308440
  17.2 27.1 %shard_map.113 = bf16[16,16,2688]{2,1,0:T(8,128)(2,1)S(1)} custom-call(bf16[16,2688]{1,0:T(8,128)(2,1)S(1)} %pad.231.shard_ref), custom_call_target="tpu_custom_call" | custom-call | tf_op jit(solution)/shard_map/pallas_call | solution.py:91
  44.5 0.8 copy.27
  45.3 0.6 fusion.292
  47.2 0.7 and_select_fusion
  47.9 0.6 fusion.291
  52.3 2.1 %constant_dynamic-slice_fusion.1 = (bf16[1,96,2592]{2,0,1:T(2,128)(2,1)S(1)}, bf16[1,96,2592]{2,0,1:T(2,128)(2,1)S(1)}) fusion(bf16[2,96,2592]{2,0,1:T(2,128)(2,1)S(1)} %bitcast.77, s32[]{:T(128)S(6)} %select_n.1857, s32[]{:T(128)S(6)} %select_n.1889), kind=kLoop, calls=%fused_computation.474 | loop fusion | bytes 1990664 | tf_op jit(solution)/shard_map/jit(dynamic_index_in_dim)/dynamic_slice | solution.py:357
  54.6 3.7 %convolution_bitcast_fusion.2 = f32[1,96,1024]{2,1,0:T(8,128)S(1)} fusion(bf16[96,2592]{1,0:T(8,128)(2,1)S(1)} %get-tuple-element.127, bf16[2592,1024]{1,0:T(8,128)(2,1)} %copy-done.3), kind=kOutput, calls=%fused_computation.6 | convolution fusion | flops 509607936 | bytes 6199296 | tf_op jit(solution)/shard_map/dot_general | solution.py:358
  58.4 1.0 convolution_bitcast_fusion.3
  59.4 0.7 compare_and_fusion
  60.4 1.9 %convolution_bitcast_fusion = f32[1,96,2592]{2,1,0:T(8,128)S(1)} fusion(bf16[2592,1024]{1,0:T(8,128)(2,1)S(1)} %bitcast.76, bf16[2,96,1024]{2,1,0:T(8,128)(2,1)S(1)} %fusion.243), kind=kOutput, calls=%fused_computation.1 | convolution fusion | flops 509607936 | bytes 6500352 | tf_op jit(solution)/shard_map/dot_general | solution.py:370
  62.4 1.8 %convolution_bitcast_fusion.1 = f32[1,96,2592]{2,1,0:T(8,128)S(1)} fusion(bf16[2592,1024]{1,0:T(8,128)(2,1)S(1)} %bitcast.74, bf16[2,96,1024]{2,1,0:T(8,128)(2,1)S(1)} %fusion.243), kind=kOutput, calls=%fused_computation.2 | convolution fusion | flops 509607936 | bytes 6500352 | tf_op jit(solution)/shard_map/dot_general | solution.py:370
  64.3 5.8 %convolution_convert_fusion = bf16[96,2592,2]{1,2,0:T(2,128)(2,1)S(1)} fusion(f32[2,96,2592]{2,1,0:T(8,128)S(1)} %maximum_multiply_fusion, pred[2,1]{0,1:T(4,128)(4,1)S(1)} %get-tuple-element.125, pred[2,1]{0,1:T(4,128)(4,1)S(1)} %get-tuple-element.126), kind=kOutput, calls=%fused_computation | convolution fusion | flops 12441604 | bytes 2985988 | tf_op jit(solution)/shard_map/sj,srk->rjk/dot_general | solution.py:378
  70.9 50.4 %shard_map.114 = f32[8,6,2592]{2,1,0:T(8,128)S(1)} custom-call(bf16[16,16,2688]{2,1,0:T(8,128)(2,1)S(1)} %pad.234.part_ref, bf16[48,16]{1,0:T(8,128)(2,1)S(1)} %pad.235.place_ref), custom_call_target="tpu_custom_call" | custom-call | tf_op jit(solution)/shard_map/pallas_call | solution.py:228
  121.3 0.9 copy.32
  122.2 0.7 fusion.231
  123.3 0.7 fusion.233
  124.4 0.6 fusion.235
  125.1 0.4 fusion.288
  125.5 2.2 %fusion.123 = f32[1,96,1024]{2,1,0:T(8,128)S(1)} fusion(f32[96,1024]{1,0:T(8,128)S(1)} %get-tuple-element.58, f32[96,1024]{1,0:T(8,128)S(1)} %get-tuple-element.57, f32[96,1024]{1,0:T(8,128)S(1)} %get-tuple-element.56, f32[96,1024]{1,0:T(8,128)S(1)} %get-tuple-element.55, f32[96,1024]{1,0:T(8,128)S(1)} %get-tuple-element.59, ...), kind=kLoop, calls=%fused_computation.243 | loop fusion | flops 5210112 | bytes 11037696 | tf_op jit(solution)/shard_map/stack | solution.py:400
  127.8 0.7 fusion.237
  128.9 0.7 fusion.239
  130.1 0.6 fusion.241
  131.2 2.2 %fusion.70 = f32[1,96,1024]{2,1,0:T(8,128)S(1)} fusion(f32[96,1024]{1,0:T(8,128)S(1)} %get-tuple-element.32, f32[96,1024]{1,0:T(8,128)S(1)} %get-tuple-element.31, f32[96,1024]{1,0:T(8,128)S(1)} %get-tuple-element.30, f32[96,1024]{1,0:T(8,128)S(1)} %get-tuple-element.29, f32[96,1024]{1,0:T(8,128)S(1)} %get-tuple-element.33, ...), kind=kLoop, calls=%fused_computation.190 | loop fusion | flops 5210112 | bytes 11037696 | tf_op jit(solution)/shard_map/stack | solution.py:400
  133.5 0.7 multiply_reduce_fusion
  135.6 1.1 fusion.11
  (130 shorter events, 10.5 us)
Async XLA Ops:
  0.6 1.0 copy-start
  9.8 7.1 %copy-start.11 = (bf16[8,6,2592]{2,0,1:T(8,128)(2,1)S(1)}, bf16[8,6,2592]{2,0,1:T(8,128)(2,1)}, u32[]{:S(2)}) copy-start(bf16[8,6,2592]{2,0,1:T(8,128)(2,1)} %param.17) | copy-start | bytes 746500
  9.8 7.1 %copy-start.15 = (s32[1,2]{1,0:T(1,128)S(1)}, s32[1,2]{1,0:T(1,128)}, u32[]{:S(2)}) copy-start(s32[1,2]{1,0:T(1,128)} %param.18) | copy-start | bytes 28
  11.3 34.0 %copy-start.14 = (s32[1,2]{1,0:T(1,128)S(1)}, s32[1,2]{1,0:T(1,128)}, u32[]{:S(2)}) copy-start(s32[1,2]{1,0:T(1,128)} %param.19) | copy-start | bytes 28
  12.1 2.4 %copy-start.2 = (bf16[2592,1024]{1,0:T(8,128)(2,1)}, bf16[2592,1024]{1,0:T(8,128)(2,1)S(1)}, u32[]{:S(2)}) copy-start(bf16[2592,1024]{1,0:T(8,128)(2,1)S(1)} %get-tuple-element.69) | copy-start | bytes 15925252
  14.5 2.4 %copy-start.3 = (bf16[2592,1024]{1,0:T(8,128)(2,1)}, bf16[2592,1024]{1,0:T(8,128)(2,1)S(1)}, u32[]{:S(2)}) copy-start(bf16[2592,1024]{1,0:T(8,128)(2,1)S(1)} %get-tuple-element.70) | copy-start | bytes 15925252
  52.3 6.0 %slice-start = ((s8[5308416]{0:T(1024)(128)(4,1)}), s8[4194304]{0:T(1024)(128)(4,1)S(1)}, s32[]{:S(2)}) async-start(s8[5308416]{0:T(1024)(128)(4,1)} %bitcast.73), calls=%async_computation | async-start | bytes 8388608
  54.5 3.9 %slice-start.1 = ((s8[5308416]{0:T(1024)(128)(4,1)}), s8[1114112]{0:T(1024)(128)(4,1)S(1)}, s32[]{:S(2)}) async-start(s8[5308416]{0:T(1024)(128)(4,1)} %bitcast.73), calls=%async_computation.1 | async-start | bytes 2228224
  54.6 5.5 %copy-start.16 = (f32[2]{0:T(128)S(1)}, f32[2]{0:T(128)}, u32[]{:S(2)}) copy-start(f32[2]{0:T(128)} %param.12) | copy-start | bytes 28
  54.6 5.6 %copy-start.4 = (bf16[2,96,1024]{2,1,0:T(8,128)(2,1)S(1)}, bf16[2,96,1024]{2,1,0:T(8,128)(2,1)}, u32[]{:S(2)}) copy-start(bf16[2,96,1024]{2,1,0:T(8,128)(2,1)} %param.10) | copy-start | bytes 1179652
  54.6 5.6 %copy-start.9 = (bf16[2,96,1024]{2,1,0:T(8,128)(2,1)S(1)}, bf16[2,96,1024]{2,1,0:T(8,128)(2,1)}, u32[]{:S(2)}) copy-start(bf16[2,96,1024]{2,1,0:T(8,128)(2,1)} %param.11) | copy-start | bytes 1179652
  54.6 5.8 %slice-start.2 = ((s8[5308416]{0:T(1024)(128)(4,1)}), s8[4194304]{0:T(1024)(128)(4,1)S(1)}, s32[]{:S(2)}) async-start(s8[5308416]{0:T(1024)(128)(4,1)} %bitcast.75), calls=%async_computation.2 | async-start | bytes 8388608
  58.4 1.8 %copy-start.5 = (f32[1,96,1024]{2,1,0:T(8,128)}, f32[1,96,1024]{2,1,0:T(8,128)S(1)}, u32[]{:S(2)}) copy-start(f32[1,96,1024]{2,1,0:T(8,128)S(1)} %convolution_bitcast_fusion.2) | copy-start | bytes 1179652
  58.4 2.0 %slice-start.3 = ((s8[5308416]{0:T(1024)(128)(4,1)}), s8[1114112]{0:T(1024)(128)(4,1)S(1)}, s32[]{:S(2)}) async-start(s8[5308416]{0:T(1024)(128)(4,1)} %bitcast.75), calls=%async_computation.3 | async-start | bytes 2228224
  59.4 0.8 copy-start.7
  131.2 2.3 %copy-start.12 = (f32[96]{0:T(128)S(1)}, f32[96]{0:T(128)}, u32[]{:S(2)}) copy-start(f32[96]{0:T(128)} %param.16) | copy-start | bytes 1156
  131.2 2.3 %copy-start.13 = (f32[96]{0:T(128)S(1)}, f32[96]{0:T(128)}, u32[]{:S(2)}) copy-start(f32[96]{0:T(128)} %param.15) | copy-start | bytes 1156
  131.2 4.3 %copy-start.6 = (f32[1,96,1024]{2,1,0:T(8,128)S(1)}, f32[1,96,1024]{2,1,0:T(8,128)}, u32[]{:S(2)}) copy-start(f32[1,96,1024]{2,1,0:T(8,128)} %copy-done.5) | copy-start | bytes 1179652
  131.2 4.3 %copy-start.8 = (f32[1,96,1024]{2,1,0:T(8,128)S(1)}, f32[1,96,1024]{2,1,0:T(8,128)}, u32[]{:S(2)}) copy-start(f32[1,96,1024]{2,1,0:T(8,128)} %copy-done.7) | copy-start | bytes 1179652
  131.2 4.3 %copy-start.10 = (bf16[2,96,1024]{2,1,0:T(8,128)(2,1)S(1)}, bf16[2,96,1024]{2,1,0:T(8,128)(2,1)}, u32[]{:S(2)}) copy-start(bf16[2,96,1024]{2,1,0:T(8,128)(2,1)} %param.11) | copy-start | bytes 1179652
  131.2 5.5 %copy-start.1 = (f32[1000,96]{0,1:T(8,128)S(1)}, f32[1000,96]{0,1:T(8,128)}, u32[]{:S(2)}) copy-start(f32[1000,96]{0,1:T(8,128)} %param.14) | copy-start | bytes 1152004

commit v2 on v0

v2 whole, which is shorter than its diff:
```python
import functools

import jax
import jax.numpy as jnp
import numpy as np
from jax import lax
from jax.experimental import pallas as pl
from jax.experimental.pallas import tpu as pltpu
from jax.sharding import PartitionSpec as P

GROUPS = 32
SIDE = 16
DEPTH = 4
EPSILON = 1e-05
MESH = pl.DeviceIdType.MESH
RING = 8
C = 96
CELLS = 1024
PLANE = SIDE * SIDE
SPAN = 864
WIDE = 896
TILES = WIDE // 128
ROWS = 36
PACK = (32, WIDE + 128)
BLOCK = 48
OUT_TILES = 64
SHIFTS = [(dy, dz) for dy in (-1, 0, 1) for dz in (-1, 0, 1)]
HOPS = {(0, 0): 4, (0, 1): 3, (1, 0): 3, (1, 1): 4}
F32 = jnp.float32
BF16 = jnp.bfloat16


def bases(first):
    out = {}
    for key, hops in HOPS.items():
        out[key] = first
        first += hops
    return out


def constants():
    main = np.zeros((576, 512), np.float32)
    last = np.zeros((576, 256), np.float32)
    spread = np.zeros((16 * 40, 576), np.float32)
    for s in range(16):
        for q in range(ROWS):
            j, dx, r = q // 18, q % 18 // 6, q % 6
            row = j * 288 + dx * C + 6 * s + r
            if q < 32:
                main[row, 32 * s + q] = 1
            else:
                last[row, 16 * s + q - 32] = 1
                spread[40 * s + q + 4, row] = 1
            spread[40 * s + q, row] = 1
    group = np.kron(np.eye(GROUPS, dtype=np.float32), np.ones((3, 3), np.float32))
    return main, last, spread, group


def rcopy(src, dst, sems, at, device_id):
    return pltpu.make_async_remote_copy(
        src_ref=src,
        dst_ref=dst,
        send_sem=sems[0].at[at],
        recv_sem=sems[1].at[at],
        device_id=device_id,
        device_id_type=MESH,
    )


def column_of(row, eye):
    return jnp.sum(eye * row, axis=1, keepdims=True)


def inside(lane, dy, dz):
    row = lane // SIDE % SIDE
    col = lane % SIDE
    ok = None
    for at, step in ((row, dy), (col, dz)):
        if step != 0:
            one = (at + step >= 0) & (at + step < SIDE)
            ok = one if ok is None else ok & one
    return ok


def pack(rows40):
    half = lax.broadcasted_iota(jnp.int32, (8, 128), 0) < 4
    tail = [rows40[32:40, t * 128 : (t + 1) * 128] for t in range(TILES)] + [
        jnp.zeros((8, 128), F32)
    ]
    last = [jnp.where(half, tail[t], tail[t + 1]) for t in range(0, 8, 2)]
    packed = jnp.concatenate([rows40[:32], jnp.concatenate(last, axis=0)], axis=1)
    return packed.astype(BF16)


def unpack_last(last):
    last = last.astype(F32)
    keep = lax.broadcasted_iota(jnp.int32, (16, 128), 0) < 4
    pieces = []
    for t in range(TILES):
        rolled = last if t == 0 else pltpu.roll(last, 32 - 4 * t, 0)
        pieces.append(jnp.where(keep, rolled[:16], 0.0))
    return jnp.concatenate(pieces, axis=1).astype(BF16)


def kernel(
    chips,
    lat_ref, tgt_ref, reward_ref, step_ref, time_ref, gain_ref, bias_ref, weight_ref, pair_ref,
    count_ref, main_ref, last_ref, spread_ref, group_ref,
    gw_ref, gi_ref,
    got, normed, slope, rstd, cols, both, ups, ucat, fold, part, held, stage, total, swap_out,
    swap_in, table, core_in, half, chunk_in, full,
    ag_s, ag_r, rs_s, rs_r, dp_s, dp_r,
):
    f = lax.axis_index("fsdp")
    z = f // 2
    x = f % 2
    nbr = z * 2 + 1 - x
    up = lax.rem(z + 1, RING) * 2 + x
    down = lax.rem(z + RING - 1, RING) * 2 + x
    d = lax.axis_index("dp")
    core = d % 2
    chip = d // 2
    twin = chip * 2 + 1 - core
    peers = [lax.rem(chip + i, chips) for i in range(1, chips)]
    barrier = pltpu.get_barrier_semaphore()
    for other in (nbr, up, down):
        pl.semaphore_signal(barrier, inc=1, device_id={"fsdp": other}, device_id_type=MESH)
    pl.semaphore_signal(barrier, inc=1, device_id={"dp": twin}, device_id_type=MESH)
    for peer in peers:
        pl.semaphore_signal(
            barrier, inc=1, device_id={"dp": peer * 2 + core}, device_id_type=MESH
        )

    rows = []
    for j in range(2):
        mine = weight_ref[pair_ref[0, j]].astype(F32)
        for dx in range(3):
            rows.append(mine[:, dx * SPAN : (dx + 1) * SPAN])
    stacked = jnp.concatenate(rows, axis=0)
    stacked = jnp.concatenate([stacked, stacked[32:36]], axis=0)
    stacked = jnp.concatenate([stacked, jnp.zeros((40, WIDE - SPAN), F32)], axis=1)
    got[f] = pack(stacked)
    pl.semaphore_wait(barrier, 4 + len(peers))

    ag = (ag_s, ag_r)
    ag_base = bases(1)
    ag_copies = {key: [] for key in HOPS}

    def ag_send(key, h):
        col, direction = key
        zz = lax.rem(z + RING - h, RING) if direction == 0 else lax.rem(z + h, RING)
        item = zz * 2 + (x if col == 0 else 1 - x)
        copy = rcopy(
            got.at[item], got.at[item], ag, ag_base[key] + h,
            {"fsdp": up if direction == 0 else down},
        )
        copy.start()
        ag_copies[key].append(copy)

    def ag_hop(h):
        for key, hops in HOPS.items():
            if h <= hops:
                ag_copies[key][h - 1].wait_recv()
            if h < hops:
                ag_send(key, h)

    swap = rcopy(got.at[f], got.at[f], ag, 0, {"fsdp": nbr})
    swap.start()
    ag_send((0, 0), 0)
    ag_send((0, 1), 0)

    eye = (
        lax.broadcasted_iota(jnp.int32, (C, C), 0) == lax.broadcasted_iota(jnp.int32, (C, C), 1)
    ).astype(F32)
    gain = column_of(gain_ref[...], eye)
    bias = column_of(bias_ref[...], eye)
    lane = lax.broadcasted_iota(jnp.int32, (C, CELLS), 1)

    def group_mean(field):
        sums = jnp.broadcast_to(jnp.sum(field, axis=1, keepdims=True), (C, 128))
        spread = jnp.dot(
            group_ref[...], sums, precision=lax.Precision.HIGHEST, preferred_element_type=F32
        )
        return spread[:, :1] * (1.0 / (3 * CELLS))

    def norm(i):
        start = lat_ref[i].astype(F32) + column_of(time_ref[pl.ds(step_ref[i], 1), :], eye)
        centred = start - group_mean(start)
        scale = lax.rsqrt(group_mean(centred * centred) + EPSILON)
        value = centred * scale
        pre = value * gain + bias
        sig = 1.0 / (1.0 + jnp.exp(-pre))
        normed[i] = value
        slope[i] = sig * (1.0 + pre * (1.0 - sig)) * gain
        rstd[i] = jnp.broadcast_to(scale, (C, 128))
        fold[...] = (pre * sig).astype(BF16).astype(F32)

    def unfold(i):
        act = fold[...]
        for at, (dy, dz) in enumerate(SHIFTS):
            move = 16 * dy + dz
            value = act
            if move != 0:
                value = jnp.where(
                    inside(lane, dy, dz), pltpu.roll(act, (-move) % CELLS, 1), 0.0
                )
            cols[i, at * C : (at + 1) * C, :] = value.astype(BF16)
        cols[i, SPAN:WIDE, :] = jnp.zeros((WIDE - SPAN, CELLS), BF16)

    norm(0)
    swap.wait_recv()
    ag_send((1, 0), 0)
    ag_send((1, 1), 0)
    ag_hop(1)
    unfold(0)
    ag_hop(2)
    norm(1)
    ag_hop(3)
    unfold(1)
    ag_hop(4)
    swap.wait_send()
    for key in HOPS:
        for copy in ag_copies[key]:
            copy.wait_send()

    main = got[:, :, :WIDE].reshape(512, WIDE)
    tails = jnp.concatenate([unpack_last(got[s, :, WIDE:]) for s in range(16)], axis=0)
    kernels = jnp.dot(main_ref[...], main, preferred_element_type=F32) + jnp.dot(
        last_ref[...], tails, preferred_element_type=F32
    )
    both[...] = kernels.astype(BF16).reshape(2, 288, WIDE)

    first, second = count_ref[0, 0], count_ref[0, 1]
    which = []
    grads = []
    zero = jnp.zeros((C, PLANE), F32)
    for i in range(2):
        place = f * 2 + i
        in_first = place < first
        in_second = (place >= first) & (place < first + second)
        which.append(in_second.astype(jnp.int32))
        live = jnp.where(in_first | in_second, reward_ref[i], 0.0)
        taps = jnp.dot(both[which[i]], cols[i], preferred_element_type=F32)
        mixed = (
            jnp.concatenate([zero, taps[:C, :-PLANE]], axis=1)
            + taps[C : 2 * C]
            + jnp.concatenate([taps[2 * C :, PLANE:], zero], axis=1)
        )
        upstream = live * (lat_ref[i].astype(F32) + mixed - tgt_ref[i].astype(F32))
        ups[i] = upstream
        rounded = upstream.astype(BF16)
        none = jnp.zeros((C, PLANE), BF16)
        ucat[i, :C] = jnp.concatenate([rounded[:, PLANE:], none], axis=1)
        ucat[i, C : 2 * C] = rounded
        ucat[i, 2 * C :] = jnp.concatenate([none, rounded[:, :-PLANE]], axis=1)
        grad = lax.dot_general(
            ucat[i], cols[i], (((1,), (1,)), ((), ())), preferred_element_type=F32
        )
        grads.append(
            (
                grad * (jnp.where(in_first, 1.0, 0.0) / CELLS),
                grad * (jnp.where(in_second, 1.0, 0.0) / CELLS),
            )
        )
    sums = jnp.concatenate(
        [(grads[0][j] + grads[1][j]).astype(BF16) for j in range(2)], axis=0
    )
    for block in range(4):
        spread = jnp.dot(
            spread_ref[block * 160 : (block + 1) * 160, :], sums, preferred_element_type=F32
        )
        for s in range(4):
            part[block * 4 + s] = pack(spread[s * 40 : (s + 1) * 40])

    rs = (rs_s, rs_r)
    rs_base = bases(0)
    rs_copies = {key: [] for key in HOPS}

    def rs_hop(h):
        for key, hops in HOPS.items():
            if h >= hops:
                continue
            col, direction = key
            away = hops - h
            zz = lax.rem(z + away, RING) if direction == 0 else lax.rem(z + RING - away, RING)
            at = rs_base[key] + h
            if h == 0:
                src = part.at[zz * 2 + col]
            else:
                rs_copies[key][h - 1].wait_recv()
                stage[at] = (
                    held[at - 1].astype(F32) + part[zz * 2 + col].astype(F32)
                ).astype(BF16)
                src = stage.at[at]
            copy = rcopy(src, held.at[at], rs, at, {"fsdp": up if direction == 0 else down})
            copy.start()
            rs_copies[key].append(copy)

    def back(i):
        products = lax.dot_general(
            both[which[i]], ucat[i], (((0,), (0,)), ((), ())), preferred_element_type=F32
        )
        acc = products[4 * C : 5 * C]
        for at, (dy, dz) in enumerate(SHIFTS):
            move = 16 * dy + dz
            if move != 0:
                piece = products[at * C : (at + 1) * C]
                acc = acc + jnp.where(
                    inside(lane, -dy, -dz), pltpu.roll(piece, move % CELLS, 1), 0.0
                )
        fold[...] = acc

    def finish(i):
        value = normed[i]
        flow = fold[...] * slope[i]
        start = rstd[i][:, :1] * (flow - group_mean(flow) - value * group_mean(flow * value))
        gi_ref[i] = (ups[i] + start).astype(BF16)

    rs_hop(0)
    back(0)
    rs_hop(1)
    finish(0)
    rs_hop(2)
    back(1)
    rs_hop(3)
    finish(1)
    for col in (0, 1):
        rs_copies[(col, 0)][-1].wait_recv()
        rs_copies[(col, 1)][-1].wait_recv()
        value = (
            part[z * 2 + col].astype(F32)
            + held[rs_base[(col, 0)] + HOPS[(col, 0)] - 1].astype(F32)
            + held[rs_base[(col, 1)] + HOPS[(col, 1)] - 1].astype(F32)
        )
        total[col] = value
        swap_out[col] = value.astype(BF16)
    cross = rcopy(swap_out.at[1 - x], swap_in, rs, 14, {"fsdp": nbr})
    cross.start()
    cross.wait_recv()
    lane_sum = (total[x] + swap_in[...].astype(F32)).astype(BF16)
    lane_sum = jnp.concatenate([lane_sum[:, :WIDE], unpack_last(lane_sum[:, WIDE:])], axis=0)
    row = lax.broadcasted_iota(jnp.int32, (144, BLOCK), 0)
    col = lax.broadcasted_iota(jnp.int32, (144, BLOCK), 1)
    ahead = jnp.where(col < 18, pair_ref[0, 0] * 18, pair_ref[0, 1] * 18 - 18)
    choose = ((row - col == ahead) & (col < ROWS)).astype(F32).astype(BF16)
    wide = jnp.dot(choose, lane_sum, preferred_element_type=F32).astype(BF16)
    for r in range(9):
        for t in range(TILES):
            table[r * TILES + t] = wide[r * 16 : (r + 1) * 16, t * 128 : (t + 1) * 128]
    table[OUT_TILES - 1] = jnp.zeros((16, 128), BF16)

    dp = (dp_s, dp_r)
    own_half = OUT_TILES // 2
    share = own_half // chips
    first_tile = core * own_half
    pair = rcopy(
        table.at[pl.ds(own_half - first_tile, own_half)], core_in, dp, 30, {"dp": twin}
    )
    pair.start()
    pair.wait_recv()
    half[...] = (
        table[pl.ds(first_tile, own_half)].astype(F32) + core_in[...].astype(F32)
    ).astype(BF16)
    scatters = []
    for i, peer in enumerate(peers):
        copy = rcopy(
            half.at[pl.ds(peer * share, share)], chunk_in.at[i], dp, i,
            {"dp": peer * 2 + core},
        )
        copy.start()
        scatters.append(copy)
    acc = half[pl.ds(chip * share, share)].astype(F32)
    for i, copy in enumerate(scatters):
        copy.wait_recv()
        acc = acc + chunk_in[i].astype(F32)
    own = pl.ds(first_tile + chip * share, share)
    full[own] = acc.astype(BF16)
    gathers = []
    for i, peer in enumerate(peers):
        copy = rcopy(full.at[own], full.at[own], dp, 15 + i, {"dp": peer * 2 + core})
        copy.start()
        gathers.append(copy)
    for copy in gathers:
        copy.wait_recv()
    mine = pl.ds(first_tile, own_half)
    last = rcopy(full.at[mine], full.at[mine], dp, 31, {"dp": twin})
    last.start()
    last.wait_recv()
    lines = jnp.concatenate(
        [
            jnp.concatenate([full[r * TILES + t].astype(F32) for t in range(TILES)], axis=1)
            for r in range(9)
        ],
        axis=0,
    )
    for e in range(8):
        for dx in range(3):
            at = e * 18 + dx * 6
            gw_ref[e, :, dx * SPAN : (dx + 1) * SPAN] = lines[at : at + 6, :SPAN]
    for key in HOPS:
        for copy in rs_copies[key]:
            copy.wait_send()
    for copy in [cross, pair, last] + scatters + gathers:
        copy.wait_send()


def local(
    chips,
    latents,
    targets,
    rewards,
    time_steps,
    time_table,
    norm_gain,
    norm_bias,
    expert_weights,
    lane_experts,
    lane_counts,
):
    main, last, spread, group = constants()
    vmem = pl.BlockSpec(memory_space=pltpu.VMEM)
    smem = pl.BlockSpec(memory_space=pltpu.SMEM)
    sems = pltpu.SemaphoreType.DMA
    return pl.pallas_call(
        functools.partial(kernel, chips),
        out_shape=(
            jax.ShapeDtypeStruct((8, 6, 3 * SPAN), F32),
            jax.ShapeDtypeStruct((2, C, CELLS), BF16),
        ),
        in_specs=[vmem, vmem, smem, smem, vmem, vmem, vmem, vmem, smem, smem] + [vmem] * 4,
        out_specs=(vmem, vmem),
        scratch_shapes=[
            pltpu.VMEM((16,) + PACK, BF16),
            pltpu.VMEM((2, C, CELLS), F32),
            pltpu.VMEM((2, C, CELLS), F32),
            pltpu.VMEM((2, C, 128), F32),
            pltpu.VMEM((2, WIDE, CELLS), BF16),
            pltpu.VMEM((2, 288, WIDE), BF16),
            pltpu.VMEM((2, C, CELLS), F32),
            pltpu.VMEM((2, 288, CELLS), BF16),
            pltpu.VMEM((C, CELLS), F32),
            pltpu.VMEM((16,) + PACK, BF16),
            pltpu.VMEM((14,) + PACK, BF16),
            pltpu.VMEM((14,) + PACK, BF16),
            pltpu.VMEM((2,) + PACK, F32),
            pltpu.VMEM((2,) + PACK, BF16),
            pltpu.VMEM(PACK, BF16),
            pltpu.VMEM((OUT_TILES, 16, 128), BF16),
            pltpu.VMEM((OUT_TILES // 2, 16, 128), BF16),
            pltpu.VMEM((OUT_TILES // 2, 16, 128), BF16),
            pltpu.VMEM((15, OUT_TILES // 2 // chips, 16, 128), BF16),
            pltpu.VMEM((OUT_TILES, 16, 128), BF16),
            sems((15,)),
            sems((15,)),
            sems((15,)),
            sems((15,)),
            sems((32,)),
            sems((32,)),
        ],
        compiler_params=pltpu.CompilerParams(
            collective_id=0, has_side_effects=True, vmem_limit_bytes=50 * 2**20
        ),
    )(
        latents, targets, rewards, time_steps, time_table, norm_gain[None, :],
        norm_bias[None, :], expert_weights, lane_experts, lane_counts,
        jnp.asarray(main, BF16), jnp.asarray(last, BF16), jnp.asarray(spread, BF16),
        jnp.asarray(group, F32),
    )


def solution(mesh):
    placed = (
        P(("dp", "fsdp"), None, None),
        P(("dp", "fsdp"), None, None),
        P(("dp", "fsdp")),
        P(("dp", "fsdp")),
        P(),
        P(),
        P(),
        P(None, "fsdp", None),
        P("dp", None),
        P("dp", None),
    )
    return jax.shard_map(
        functools.partial(local, mesh.shape["dp"] // 2),
        mesh=mesh,
        in_specs=placed,
        out_specs=(P(None, "fsdp", None), P(("dp", "fsdp"), None, None)),
        check_vma=False,
    )
```

time: 512 us -> 85.3 us (0.17)
  waiting for transfers between devices: 402 us -> 0 us
  Pallas kernels: 0 us -> 79.3 us
  blocking collectives: 40.3 us -> 0 us
  matrix products: 20.6 us -> 0 us
  between operations: 20.6 us -> 0.81 us
  other arithmetic: 18.9 us -> 0 us
    psum x1 -> x0, waiting for transfers between devices: 278 us -> none  [local(): grad_weight = lax.psum(table.astype(jnp.bfloat16), 'dp').astype(jnp.float32)]
    unnamed x3 -> x0, waiting for transfers between devices: 124 us -> none
    pallas_call x0 -> x1, Pallas kernels: none -> 79.3 us  [local(): pl.pallas_call(functools.partial(kernel, chips), out_shape=(jax.ShapeDtyp...]
    all_gather x1 -> x0, blocking collectives: 40.3 us -> none  [local(): piece = lax.all_gather(lane_shards, 'fsdp', axis=1, tiled=True)]
    dot_general x14 -> x0, matrix products: 20.6 us -> none  [the longest x1 6.72 us: local(): jnp.einsum('sj,srk->rjk', member, stacked, precision=lax.Precision.HIGHEST)]
  transfers between devices with their start and end apart: 2 -> 0, of which waited for: 2 -> 0; matrix products, arithmetic and copies ran while one was open for 3% -> 0% of each run, Pallas kernels for 0% -> 0%
where the time goes in v2:
time: 85.3 us; the launch traced here: 85 us
  Pallas kernels  79.3 us (93%)
  local copies, waits for them, and re-layouts  4.94 us (6%)
    pallas_call x1, Pallas kernels, local(): pl.pallas_call(functools.partial(kernel, chips), out_shape=(jax.ShapeDtyp...  79.3 us
    unnamed x25, local copies, waits for them, and re-layouts  4.06 us

profile of v2, /device:TPU:1, one launch (start us, length us, event | category | flops | bytes accessed | tf_op | source)
XLA Modules:
  0.0 85.0 jit_solution(3632460252618729884)
XLA Ops:
  0.6 0.0 copy-start.1
  0.6 0.0 copy-start.2
  0.6 1.1 %copy.17.weight_ref = bf16[8,6,2592]{2,1,0:T(8,128)(2,1)S(1)} copy(bf16[8,6,2592]{2,0,1:T(8,128)(2,1)} %param.21) | data formatting | bytes 497664 | tf_op args[7]
  1.7 0.0 copy-start
  1.7 0.0 copy-start.4
  1.7 0.0 copy-start.5
  1.7 0.0 copy-start.6
  1.8 0.0 copy-start.7
  1.8 0.0 copy-start.8
  1.8 0.0 copy-start.9
  1.8 0.0 copy-start.10
  1.8 1.2 %copy.16.time_ref = f32[1000,96]{1,0:T(8,128)S(1)} copy(f32[1000,96]{0,1:T(8,128)} %param.18) | data formatting | bytes 768000 | tf_op args[4]
  3.1 0.0 copy-done.1
  3.1 0.0 copy-done.2
  3.1 0.0 copy-done
  3.1 0.0 copy-done.4
  3.1 0.0 copy-done.5
  3.1 0.0 copy-done.6
  3.1 0.0 copy-done.7
  3.1 0.0 copy-done.8
  3.1 0.0 copy-done.9
  3.1 0.0 copy-done.10
  3.2 0.0 copy-start.3
  3.2 1.0 %copy-done.3 = bf16[576,256]{1,0:T(8,128)(2,1)S(1)} copy-done((bf16[576,256]{1,0:T(8,128)(2,1)S(1)}, bf16[576,256]{1,0:T(8,128)(2,1)}, u32[]{:S(2)}) %copy-start.3) | copy-done | bytes 294936
  4.1 79.3 %shard_map.149 = (f32[8,6,2592]{2,1,0:T(8,128)S(1)}, bf16[2,96,1024]{2,1,0:T(8,128)(2,1)S(1)}) custom-call(bf16[2,96,1024]{2,1,0:T(8,128)(2,1)S(1)} %copy-done.1, bf16[2,96,1024]{2,1,0:T(8,128)(2,1)S(1)} %copy-done.2, f32[2]{0:T(128)S(1)} %copy-done.5, s32[2]{0:T(128)S(1)} %copy-done.6, f32[1000,96]{1,0:T(8,128)S(1)} %copy.16.time_ref, f32[1,96]{1,0:T(1,128)S(1)} %bitcast.2, ...), custom_call_target="tpu_custom_call" | custom-call | tf_op jit(solution)/shard_map/pallas_call | solution.py:424
  83.4 0.9 %copy.18 = f32[8,6,2592]{2,0,1:T(8,128)} copy(f32[8,6,2592]{2,1,0:T(8,128)S(1)} %get-tuple-element.2) | data formatting | bytes 995328 | tf_op jit(solution)/shard_map/pallas_call | solution.py:424
  84.3 0.7 copy.20
Async XLA Ops:
  0.6 2.4 %copy-start.1 = (bf16[2,96,1024]{2,1,0:T(8,128)(2,1)S(1)}, bf16[2,96,1024]{2,1,0:T(8,128)(2,1)}, u32[]{:S(2)}) copy-start(bf16[2,96,1024]{2,1,0:T(8,128)(2,1)} %lat_ref.1) | copy-start | bytes 1179652
  0.6 2.4 %copy-start.2 = (bf16[2,96,1024]{2,1,0:T(8,128)(2,1)S(1)}, bf16[2,96,1024]{2,1,0:T(8,128)(2,1)}, u32[]{:S(2)}) copy-start(bf16[2,96,1024]{2,1,0:T(8,128)(2,1)} %tgt_ref.1) | copy-start | bytes 1179652
  1.7 1.4 %copy-start = (bf16[576,512]{1,0:T(8,128)(2,1)S(1)}, bf16[576,512]{1,0:T(8,128)(2,1)}, u32[]{:S(2)}) copy-start(bf16[576,512]{1,0:T(8,128)(2,1)} %constant.8.clone.main_ref) | copy-start | bytes 1769476
  1.7 1.4 %copy-start.4 = (f32[96,96]{1,0:T(8,128)S(1)}, f32[96,96]{1,0:T(8,128)}, u32[]{:S(2)}) copy-start(f32[96,96]{1,0:T(8,128)} %constant.11.clone.group_ref) | copy-start | bytes 110596
  1.7 1.4 %copy-start.5 = (f32[2]{0:T(128)S(1)}, f32[2]{0:T(128)}, u32[]{:S(2)}) copy-start(f32[2]{0:T(128)} %reward_ref.1) | copy-start | bytes 28
  1.7 1.4 %copy-start.6 = (s32[2]{0:T(128)S(1)}, s32[2]{0:T(128)}, u32[]{:S(2)}) copy-start(s32[2]{0:T(128)} %step_ref.1) | copy-start | bytes 28
  1.8 1.4 %copy-start.7 = (f32[96]{0:T(128)S(1)}, f32[96]{0:T(128)}, u32[]{:S(2)}) copy-start(f32[96]{0:T(128)} %param.19) | copy-start | bytes 1156
  1.8 1.4 %copy-start.8 = (f32[96]{0:T(128)S(1)}, f32[96]{0:T(128)}, u32[]{:S(2)}) copy-start(f32[96]{0:T(128)} %param.20) | copy-start | bytes 1156
  1.8 1.4 %copy-start.9 = (s32[1,2]{1,0:T(1,128)S(1)}, s32[1,2]{1,0:T(1,128)}, u32[]{:S(2)}) copy-start(s32[1,2]{1,0:T(1,128)} %pair_ref.1) | copy-start | bytes 28
  1.8 1.4 %copy-start.10 = (s32[1,2]{1,0:T(1,128)S(1)}, s32[1,2]{1,0:T(1,128)}, u32[]{:S(2)}) copy-start(s32[1,2]{1,0:T(1,128)} %count_ref.1) | copy-start | bytes 28
  3.2 1.0 %copy-start.3 = (bf16[576,256]{1,0:T(8,128)(2,1)S(1)}, bf16[576,256]{1,0:T(8,128)(2,1)}, u32[]{:S(2)}) copy-start(bf16[576,256]{1,0:T(8,128)(2,1)} %constant.9.clone.last_ref) | copy-start | bytes 884740

commit v3 on v2

--- a/solution.py
+++ b/solution.py
@@ -25,17 +25,10 @@
 BLOCK = 48
 OUT_TILES = 64
 SHIFTS = [(dy, dz) for dy in (-1, 0, 1) for dz in (-1, 0, 1)]
-HOPS = {(0, 0): 4, (0, 1): 3, (1, 0): 3, (1, 1): 4}
+AWAY = (4, 3, 5, 2, 6, 1, 7)
+NEAR = (1, 7, 2, 6, 3, 5, 4)
 F32 = jnp.float32
 BF16 = jnp.bfloat16
-
-
-def bases(first):
-    out = {}
-    for key, hops in HOPS.items():
-        out[key] = first
-        first += hops
-    return out
 
 
 def constants():
@@ -44,7 +37,7 @@
     spread = np.zeros((16 * 40, 576), np.float32)
     for s in range(16):
         for q in range(ROWS):
-            j, dx, r = q // 18, q % 18 // 6, q % 6
+            dx, j, r = q // 12, q % 12 // 6, q % 6
             row = j * 288 + dx * C + 6 * s + r
             if q < 32:
                 main[row, 32 * s + q] = 1
@@ -104,70 +97,72 @@
 
 def kernel(
     chips,
-    lat_ref, tgt_ref, reward_ref, step_ref, time_ref, gain_ref, bias_ref, weight_ref, pair_ref,
-    count_ref, main_ref, last_ref, spread_ref, group_ref,
-    gw_ref, gi_ref,
-    got, normed, slope, rstd, cols, both, ups, ucat, fold, part, held, stage, total, swap_out,
-    swap_in, table, core_in, half, chunk_in, full,
-    ag_s, ag_r, rs_s, rs_r, dp_s, dp_r,
+    lat_hbm, tgt_hbm, reward_ref, step_ref, time_hbm, gain_ref, bias_ref, weight_hbm, pair_ref,
+    count_ref, main_hbm, last_hbm, spread_hbm, group_hbm,
+    gw_ref, gi_hbm,
+    gi_ref, weight_ref, lat_ref, tgt_ref, time_ref, main_ref, last_ref, spread_ref, group_ref,
+    got, normed, slope, rstd, cols, both, ups, ucat, fold, part, x_in, held, stage, table,
+    core_in, half, chunk_in, full,
+    ag_s, ag_r, rs_s, rs_r, dp_s, dp_r, in_s,
 ):
     f = lax.axis_index("fsdp")
     z = f // 2
     x = f % 2
     nbr = z * 2 + 1 - x
-    up = lax.rem(z + 1, RING) * 2 + x
-    down = lax.rem(z + RING - 1, RING) * 2 + x
     d = lax.axis_index("dp")
     core = d % 2
     chip = d // 2
     twin = chip * 2 + 1 - core
     peers = [lax.rem(chip + i, chips) for i in range(1, chips)]
+    ring = {k: lax.rem(z + k, RING) for k in range(RING)}
     barrier = pltpu.get_barrier_semaphore()
-    for other in (nbr, up, down):
+    for other in [nbr] + [ring[k] * 2 + x for k in NEAR]:
         pl.semaphore_signal(barrier, inc=1, device_id={"fsdp": other}, device_id_type=MESH)
     pl.semaphore_signal(barrier, inc=1, device_id={"dp": twin}, device_id_type=MESH)
     for peer in peers:
         pl.semaphore_signal(
             barrier, inc=1, device_id={"dp": peer * 2 + core}, device_id_type=MESH
         )
-
-    rows = []
-    for j in range(2):
-        mine = weight_ref[pair_ref[0, j]].astype(F32)
-        for dx in range(3):
-            rows.append(mine[:, dx * SPAN : (dx + 1) * SPAN])
+    inputs = {}
+    for at, (name, src, dst) in enumerate((
+        ("weight", weight_hbm, weight_ref), ("lat", lat_hbm, lat_ref), ("time", time_hbm, time_ref), ("group", group_hbm, group_ref),
+        ("main", main_hbm, main_ref), ("last", last_hbm, last_ref), ("tgt", tgt_hbm, tgt_ref),
+        ("spread", spread_hbm, spread_ref),
+    )):
+        inputs[name] = pltpu.make_async_copy(src, dst, in_s.at[at])
+        inputs[name].start()
+
+    row = lax.broadcasted_iota(jnp.int32, (16, 48), 0)
+    col = lax.broadcasted_iota(jnp.int32, (16, 48), 1)
+    expert = jnp.where(row < 6, pair_ref[0, 0], pair_ref[0, 1] - 48)
+    pick = ((col - 8 * row == expert) & (row < 12)).astype(F32).astype(BF16)
+    inputs["weight"].wait()
+    mine = jnp.dot(pick, weight_ref[...], preferred_element_type=F32)[:12]
+    rows = [mine[:, dx * SPAN : (dx + 1) * SPAN] for dx in range(3)]
+    rows.append(rows[2][8:12])
     stacked = jnp.concatenate(rows, axis=0)
-    stacked = jnp.concatenate([stacked, stacked[32:36]], axis=0)
     stacked = jnp.concatenate([stacked, jnp.zeros((40, WIDE - SPAN), F32)], axis=1)
     got[f] = pack(stacked)
-    pl.semaphore_wait(barrier, 4 + len(peers))
+    pl.semaphore_wait(barrier, RING + 1 + len(peers))
 
     ag = (ag_s, ag_r)
-    ag_base = bases(1)
-    ag_copies = {key: [] for key in HOPS}
-
-    def ag_send(key, h):
-        col, direction = key
-        zz = lax.rem(z + RING - h, RING) if direction == 0 else lax.rem(z + h, RING)
-        item = zz * 2 + (x if col == 0 else 1 - x)
-        copy = rcopy(
-            got.at[item], got.at[item], ag, ag_base[key] + h,
-            {"fsdp": up if direction == 0 else down},
-        )
+    swap = rcopy(got.at[f], got.at[f], ag, 7, {"fsdp": nbr})
+    direct = []
+    for i, k in enumerate(NEAR):
+        copy = rcopy(got.at[f], got.at[f], ag, i, {"fsdp": ring[k] * 2 + x})
         copy.start()
-        ag_copies[key].append(copy)
-
-    def ag_hop(h):
-        for key, hops in HOPS.items():
-            if h <= hops:
-                ag_copies[key][h - 1].wait_recv()
-            if h < hops:
-                ag_send(key, h)
-
-    swap = rcopy(got.at[f], got.at[f], ag, 0, {"fsdp": nbr})
-    swap.start()
-    ag_send((0, 0), 0)
-    ag_send((0, 1), 0)
+        direct.append(copy)
+        if i == 1:
+            swap.start()
+    passed = []
+
+    def hand_on(count):
+        for i in range(len(passed), len(passed) + count):
+            direct[i].wait_recv()
+            item = ring[RING - NEAR[i]] * 2 + x
+            copy = rcopy(got.at[item], got.at[item], ag, 8 + i, {"fsdp": nbr})
+            copy.start()
+            passed.append(copy)
 
     eye = (
         lax.broadcasted_iota(jnp.int32, (C, C), 0) == lax.broadcasted_iota(jnp.int32, (C, C), 1)
@@ -175,6 +170,7 @@
     gain = column_of(gain_ref[...], eye)
     bias = column_of(bias_ref[...], eye)
     lane = lax.broadcasted_iota(jnp.int32, (C, CELLS), 1)
+    moment = lax.broadcasted_iota(jnp.int32, time_ref.shape, 1)
 
     def group_mean(field):
         sums = jnp.broadcast_to(jnp.sum(field, axis=1, keepdims=True), (C, 128))
@@ -184,7 +180,9 @@
         return spread[:, :1] * (1.0 / (3 * CELLS))
 
     def norm(i):
-        start = lat_ref[i].astype(F32) + column_of(time_ref[pl.ds(step_ref[i], 1), :], eye)
+        start = lat_ref[i].astype(F32) + jnp.sum(
+            jnp.where(moment == step_ref[i], time_ref[...], 0.0), axis=1, keepdims=True
+        )
         centred = start - group_mean(start)
         scale = lax.rsqrt(group_mean(centred * centred) + EPSILON)
         value = centred * scale
@@ -207,21 +205,21 @@
             cols[i, at * C : (at + 1) * C, :] = value.astype(BF16)
         cols[i, SPAN:WIDE, :] = jnp.zeros((WIDE - SPAN, CELLS), BF16)
 
+    for name in ("lat", "time", "group"):
+        inputs[name].wait()
     norm(0)
-    swap.wait_recv()
-    ag_send((1, 0), 0)
-    ag_send((1, 1), 0)
-    ag_hop(1)
     unfold(0)
-    ag_hop(2)
+    hand_on(4)
     norm(1)
-    ag_hop(3)
+    hand_on(2)
     unfold(1)
-    ag_hop(4)
-    swap.wait_send()
-    for key in HOPS:
-        for copy in ag_copies[key]:
-            copy.wait_send()
+    hand_on(1)
+    for name in ("main", "last", "tgt", "spread"):
+        inputs[name].wait()
+    for copy in [swap] + passed:
+        copy.wait_recv()
+    for copy in [swap] + direct + passed:
+        copy.wait_send()
 
     main = got[:, :, :WIDE].reshape(512, WIDE)
     tails = jnp.concatenate([unpack_last(got[s, :, WIDE:]) for s in range(16)], axis=0)
@@ -273,28 +271,25 @@
             part[block * 4 + s] = pack(spread[s * 40 : (s + 1) * 40])
 
     rs = (rs_s, rs_r)
-    rs_base = bases(0)
-    rs_copies = {key: [] for key in HOPS}
-
-    def rs_hop(h):
-        for key, hops in HOPS.items():
-            if h >= hops:
-                continue
-            col, direction = key
-            away = hops - h
-            zz = lax.rem(z + away, RING) if direction == 0 else lax.rem(z + RING - away, RING)
-            at = rs_base[key] + h
-            if h == 0:
-                src = part.at[zz * 2 + col]
-            else:
-                rs_copies[key][h - 1].wait_recv()
-                stage[at] = (
-                    held[at - 1].astype(F32) + part[zz * 2 + col].astype(F32)
-                ).astype(BF16)
-                src = stage.at[at]
-            copy = rcopy(src, held.at[at], rs, at, {"fsdp": up if direction == 0 else down})
+    order = AWAY + (0,)
+    crosses = []
+    for i, k in enumerate(order):
+        copy = rcopy(part.at[ring[k] * 2 + 1 - x], x_in.at[i], rs, i, {"fsdp": nbr})
+        copy.start()
+        crosses.append(copy)
+    sends = []
+
+    def send_on(count):
+        for i in range(len(sends), len(sends) + count):
+            crosses[i].wait_recv()
+            stage[i] = (part[ring[AWAY[i]] * 2 + x].astype(F32) + x_in[i].astype(F32)).astype(
+                BF16
+            )
+            copy = rcopy(
+                stage.at[i], held.at[i], rs, 8 + i, {"fsdp": ring[AWAY[i]] * 2 + x}
+            )
             copy.start()
-            rs_copies[key].append(copy)
+            sends.append(copy)
 
     def back(i):
         products = lax.dot_general(
@@ -310,39 +305,36 @@
                 )
         fold[...] = acc
 
+    results = []
+
     def finish(i):
         value = normed[i]
         flow = fold[...] * slope[i]
         start = rstd[i][:, :1] * (flow - group_mean(flow) - value * group_mean(flow * value))
         gi_ref[i] = (ups[i] + start).astype(BF16)
-
-    rs_hop(0)
+        result = pltpu.make_async_copy(gi_ref.at[i], gi_hbm.at[i], in_s.at[8 + i])
+        result.start()
+        results.append(result)
+
     back(0)
-    rs_hop(1)
+    send_on(4)
     finish(0)
-    rs_hop(2)
+    send_on(3)
     back(1)
-    rs_hop(3)
     finish(1)
-    for col in (0, 1):
-        rs_copies[(col, 0)][-1].wait_recv()
-        rs_copies[(col, 1)][-1].wait_recv()
-        value = (
-            part[z * 2 + col].astype(F32)
-            + held[rs_base[(col, 0)] + HOPS[(col, 0)] - 1].astype(F32)
-            + held[rs_base[(col, 1)] + HOPS[(col, 1)] - 1].astype(F32)
-        )
-        total[col] = value
-        swap_out[col] = value.astype(BF16)
-    cross = rcopy(swap_out.at[1 - x], swap_in, rs, 14, {"fsdp": nbr})
-    cross.start()
-    cross.wait_recv()
-    lane_sum = (total[x] + swap_in[...].astype(F32)).astype(BF16)
+    crosses[7].wait_recv()
+    lane_sum = part[f].astype(F32) + x_in[7].astype(F32)
+    for i, copy in enumerate(sends):
+        copy.wait_recv()
+        lane_sum = lane_sum + held[i].astype(F32)
+    lane_sum = lane_sum.astype(BF16)
     lane_sum = jnp.concatenate([lane_sum[:, :WIDE], unpack_last(lane_sum[:, WIDE:])], axis=0)
     row = lax.broadcasted_iota(jnp.int32, (144, BLOCK), 0)
     col = lax.broadcasted_iota(jnp.int32, (144, BLOCK), 1)
-    ahead = jnp.where(col < 18, pair_ref[0, 0] * 18, pair_ref[0, 1] * 18 - 18)
-    choose = ((row - col == ahead) & (col < ROWS)).astype(F32).astype(BF16)
+    expert = jnp.where(col % 12 < 6, pair_ref[0, 0], pair_ref[0, 1])
+    choose = (
+        (row // 48 == col // 12) & (row % 48 // 8 == col % 6) & (row % 8 == expert)
+    ).astype(F32).astype(BF16)
     wide = jnp.dot(choose, lane_sum, preferred_element_type=F32).astype(BF16)
     for r in range(9):
         for t in range(TILES):
@@ -386,21 +378,17 @@
     last = rcopy(full.at[mine], full.at[mine], dp, 31, {"dp": twin})
     last.start()
     last.wait_recv()
-    lines = jnp.concatenate(
-        [
-            jnp.concatenate([full[r * TILES + t].astype(F32) for t in range(TILES)], axis=1)
-            for r in range(9)
-        ],
-        axis=0,
-    )
-    for e in range(8):
-        for dx in range(3):
-            at = e * 18 + dx * 6
-            gw_ref[e, :, dx * SPAN : (dx + 1) * SPAN] = lines[at : at + 6, :SPAN]
-    for key in HOPS:
-        for copy in rs_copies[key]:
-            copy.wait_send()
-    for copy in [cross, pair, last] + scatters + gathers:
+    for dx in range(3):
+        for r in range(6):
+            at = dx * 6 + r
+            line = jnp.concatenate(
+                [full[at // 2 * TILES + t].astype(F32)[at % 2 * 8 :][:8] for t in range(TILES)],
+                axis=1,
+            )
+            gw_ref[r, :, dx * SPAN : (dx + 1) * SPAN] = line[:, :SPAN]
+    for copy in results:
+        copy.wait()
+    for copy in crosses + sends + [pair, last] + scatters + gathers:
         copy.wait_send()
 
 
@@ -421,15 +409,25 @@
     vmem = pl.BlockSpec(memory_space=pltpu.VMEM)
     smem = pl.BlockSpec(memory_space=pltpu.SMEM)
     sems = pltpu.SemaphoreType.DMA
-    return pl.pallas_call(
+    hbm = pl.BlockSpec(memory_space=pltpu.MemorySpace.HBM)
+    grad_weight, grad_input = pl.pallas_call(
         functools.partial(kernel, chips),
         out_shape=(
-            jax.ShapeDtypeStruct((8, 6, 3 * SPAN), F32),
+            jax.ShapeDtypeStruct((6, 8, 3 * SPAN), F32),
             jax.ShapeDtypeStruct((2, C, CELLS), BF16),
         ),
-        in_specs=[vmem, vmem, smem, smem, vmem, vmem, vmem, vmem, smem, smem] + [vmem] * 4,
-        out_specs=(vmem, vmem),
+        in_specs=[hbm, hbm, smem, smem, hbm, vmem, vmem, hbm, smem, smem] + [hbm] * 4,
+        out_specs=(vmem, hbm),
         scratch_shapes=[
+            pltpu.VMEM((2, C, CELLS), BF16),
+            pltpu.VMEM((48, 3 * SPAN), BF16),
+            pltpu.VMEM((2, C, CELLS), BF16),
+            pltpu.VMEM((2, C, CELLS), BF16),
+            pltpu.VMEM(time_table.shape[::-1], F32),
+            pltpu.VMEM(main.shape, BF16),
+            pltpu.VMEM(last.shape, BF16),
+            pltpu.VMEM(spread.shape, BF16),
+            pltpu.VMEM(group.shape, F32),
             pltpu.VMEM((16,) + PACK, BF16),
             pltpu.VMEM((2, C, CELLS), F32),
             pltpu.VMEM((2, C, CELLS), F32),
@@ -440,11 +438,9 @@
             pltpu.VMEM((2, 288, CELLS), BF16),
             pltpu.VMEM((C, CELLS), F32),
             pltpu.VMEM((16,) + PACK, BF16),
-            pltpu.VMEM((14,) + PACK, BF16),
-            pltpu.VMEM((14,) + PACK, BF16),
-            pltpu.VMEM((2,) + PACK, F32),
-            pltpu.VMEM((2,) + PACK, BF16),
-            pltpu.VMEM(PACK, BF16),
+            pltpu.VMEM((8,) + PACK, BF16),
+            pltpu.VMEM((7,) + PACK, BF16),
+            pltpu.VMEM((7,) + PACK, BF16),
             pltpu.VMEM((OUT_TILES, 16, 128), BF16),
             pltpu.VMEM((OUT_TILES // 2, 16, 128), BF16),
             pltpu.VMEM((OUT_TILES // 2, 16, 128), BF16),
@@ -456,16 +452,19 @@
             sems((15,)),
             sems((32,)),
             sems((32,)),
+            sems((10,)),
         ],
         compiler_params=pltpu.CompilerParams(
-            collective_id=0, has_side_effects=True, vmem_limit_bytes=50 * 2**20
+            collective_id=0, has_side_effects=True, vmem_limit_bytes=60 * 2**20
         ),
     )(
-        latents, targets, rewards, time_steps, time_table, norm_gain[None, :],
-        norm_bias[None, :], expert_weights, lane_experts, lane_counts,
+        latents, targets, rewards, time_steps, time_table.T, norm_gain[None, :],
+        norm_bias[None, :], expert_weights.swapaxes(0, 1).reshape(48, 3 * SPAN), lane_experts,
+        lane_counts,
         jnp.asarray(main, BF16), jnp.asarray(last, BF16), jnp.asarray(spread, BF16),
         jnp.asarray(group, F32),
     )
+    return grad_weight.swapaxes(0, 1), grad_input
 
 
 def solution(mesh):

time: 85.3 us -> 76.1 us (0.89)
  Pallas kernels: 79.3 us -> 72.6 us
  local copies, waits for them, and re-layouts: 4.94 us -> 2.66 us
    pallas_call x1, Pallas kernels: 79.3 us -> 72.6 us  [local(): pl.pallas_call(functools.partial(kernel, chips), out_shape=(jax.ShapeDtyp...]
    unnamed x25 -> x4, local copies, waits for them, and re-layouts: 4.06 us -> 2.66 us
    pallas_call x1 -> x0, local copies, waits for them, and re-layouts: 0.88 us -> none  [local(): pl.pallas_call(functools.partial(kernel, chips), out_shape=(jax.ShapeDtyp...]
where the time goes in v3:
time: 76.1 us; the launch traced here: 75.9 us
  Pallas kernels  72.6 us (95%)
  local copies, waits for them, and re-layouts  2.66 us (3%)
    pallas_call x1, Pallas kernels, local(): pl.pallas_call(functools.partial(kernel, chips), out_shape=(jax.ShapeDtyp...  72.6 us
    unnamed x4, local copies, waits for them, and re-layouts  2.66 us

profile of v3, /device:TPU:1, one launch (start us, length us, event | category | flops | bytes accessed | tf_op | source)
XLA Modules:
  0.0 75.9 jit_solution(7479008801113605303)
XLA Ops:
  0.6 72.6 %shard_map.149 = (f32[6,8,2592]{2,1,0:T(8,128)}, bf16[2,96,1024]{2,1,0:T(8,128)(2,1)}) custom-call(bf16[2,96,1024]{2,1,0:T(8,128)(2,1)} %lat_hbm.1, bf16[2,96,1024]{2,1,0:T(8,128)(2,1)} %tgt_hbm.1, f32[2]{0:T(128)} %reward_ref.1, s32[2]{0:T(128)} %step_ref.1, f32[96,1000]{1,0:T(8,128)} %bitcast.8, f32[1,96]{1,0:T(1,128)} %bitcast.10, f32[1,96]{1,0:T(1,128)} %bitcast.11, ...), custom_call_target="tpu_custom_call" | custom-call | tf_op jit(solution)/shard_map/pallas_call | solution.py:413
  73.2 0.0 copy-start
  73.2 1.9 %copy.18 = f32[8,6,2592]{2,0,1:T(8,128)} copy(f32[8,6,2592]{2,0,1:T(8,128)} %bitcast.7) | data formatting | bytes 995328
  75.2 0.0 copy-done
  75.2 0.7 copy.19
Async XLA Ops:
  73.2 1.9 %copy-start = (bf16[2,96,1024]{2,1,0:T(8,128)(2,1)S(1)}, bf16[2,96,1024]{2,1,0:T(8,128)(2,1)}, u32[]{:S(2)}) copy-start(bf16[2,96,1024]{2,1,0:T(8,128)(2,1)} %get-tuple-element.9) | copy-start | bytes 1179652

commit v4 on v3

--- a/solution.py
+++ b/solution.py
@@ -25,8 +25,6 @@
 BLOCK = 48
 OUT_TILES = 64
 SHIFTS = [(dy, dz) for dy in (-1, 0, 1) for dz in (-1, 0, 1)]
-AWAY = (4, 3, 5, 2, 6, 1, 7)
-NEAR = (1, 7, 2, 6, 3, 5, 4)
 F32 = jnp.float32
 BF16 = jnp.bfloat16
 
@@ -46,7 +44,7 @@
                 spread[40 * s + q + 4, row] = 1
             spread[40 * s + q, row] = 1
     group = np.kron(np.eye(GROUPS, dtype=np.float32), np.ones((3, 3), np.float32))
-    return main, last, spread, group
+    return main, last, np.concatenate([spread, spread]), group
 
 
 def rcopy(src, dst, sems, at, device_id):
@@ -99,10 +97,10 @@
     chips,
     lat_hbm, tgt_hbm, reward_ref, step_ref, time_hbm, gain_ref, bias_ref, weight_hbm, pair_ref,
     count_ref, main_hbm, last_hbm, spread_hbm, group_hbm,
-    gw_ref, gi_hbm,
+    full, gi_hbm,
     gi_ref, weight_ref, lat_ref, tgt_ref, time_ref, main_ref, last_ref, spread_ref, group_ref,
-    got, normed, slope, rstd, cols, both, ups, ucat, fold, part, x_in, held, stage, table,
-    core_in, half, chunk_in, full,
+    got, normed, slope, rstd, cols, both, ups, ucat, fold, part, landed, stage,
+    choose_out, choose_in, lane_out, lane_in, table, chunk_in,
     ag_s, ag_r, rs_s, rs_r, dp_s, dp_r, in_s,
 ):
     f = lax.axis_index("fsdp")
@@ -116,7 +114,7 @@
     peers = [lax.rem(chip + i, chips) for i in range(1, chips)]
     ring = {k: lax.rem(z + k, RING) for k in range(RING)}
     barrier = pltpu.get_barrier_semaphore()
-    for other in [nbr] + [ring[k] * 2 + x for k in NEAR]:
+    for other in [nbr] + [ring[k] * 2 + x for k in (1, 7, 2, 6)]:
         pl.semaphore_signal(barrier, inc=1, device_id={"fsdp": other}, device_id_type=MESH)
     pl.semaphore_signal(barrier, inc=1, device_id={"dp": twin}, device_id_type=MESH)
     for peer in peers:
@@ -125,7 +123,8 @@
         )
     inputs = {}
     for at, (name, src, dst) in enumerate((
-        ("weight", weight_hbm, weight_ref), ("lat", lat_hbm, lat_ref), ("time", time_hbm, time_ref), ("group", group_hbm, group_ref),
+        ("weight", weight_hbm, weight_ref), ("lat", lat_hbm, lat_ref),
+        ("time", time_hbm, time_ref), ("group", group_hbm, group_ref),
         ("main", main_hbm, main_ref), ("last", last_hbm, last_ref), ("tgt", tgt_hbm, tgt_ref),
         ("spread", spread_hbm, spread_ref),
     )):
@@ -143,26 +142,31 @@
     stacked = jnp.concatenate(rows, axis=0)
     stacked = jnp.concatenate([stacked, jnp.zeros((40, WIDE - SPAN), F32)], axis=1)
     got[f] = pack(stacked)
-    pl.semaphore_wait(barrier, RING + 1 + len(peers))
-
-    ag = (ag_s, ag_r)
-    swap = rcopy(got.at[f], got.at[f], ag, 7, {"fsdp": nbr})
-    direct = []
-    for i, k in enumerate(NEAR):
-        copy = rcopy(got.at[f], got.at[f], ag, i, {"fsdp": ring[k] * 2 + x})
+    pl.semaphore_wait(barrier, 6 + len(peers))
+
+    row = lax.broadcasted_iota(jnp.int32, (144, BLOCK), 0)
+    col = lax.broadcasted_iota(jnp.int32, (144, BLOCK), 1)
+    expert = jnp.where(col % 12 < 6, pair_ref[0, 0], pair_ref[0, 1])
+    choose_out[...] = (
+        (row // 48 == col // 12) & (row % 48 // 8 == col % 6) & (row % 8 == expert)
+    ).astype(F32).astype(BF16)
+
+    ag_copies = {}
+
+    def pass_on(name, item, to):
+        at = len(ag_copies)
+        copy = rcopy(got.at[item], got.at[item], (ag_s, ag_r), at, {"fsdp": to})
         copy.start()
-        direct.append(copy)
-        if i == 1:
-            swap.start()
-    passed = []
-
-    def hand_on(count):
-        for i in range(len(passed), len(passed) + count):
-            direct[i].wait_recv()
-            item = ring[RING - NEAR[i]] * 2 + x
-            copy = rcopy(got.at[item], got.at[item], ag, 8 + i, {"fsdp": nbr})
-            copy.start()
-            passed.append(copy)
+        ag_copies[name] = copy
+
+    def shard(k):
+        return ring[k] * 2 + x
+
+    pass_on("swap", f, nbr)
+    for k in (2, 6, 1, 7):
+        pass_on(k, f, shard(k))
+    told = rcopy(choose_out, choose_in, (dp_s, dp_r), 32, {"dp": twin})
+    told.start()
 
     eye = (
         lax.broadcasted_iota(jnp.int32, (C, C), 0) == lax.broadcasted_iota(jnp.int32, (C, C), 1)
@@ -209,16 +213,28 @@
         inputs[name].wait()
     norm(0)
     unfold(0)
-    hand_on(4)
+    ag_copies["swap"].wait_recv()
+    pass_on("next", nbr, shard(1))
+    pass_on("previous", nbr, shard(7))
+    ag_copies[2].wait_recv()
+    pass_on(3, shard(6), shard(1))
+    ag_copies[6].wait_recv()
+    pass_on(5, shard(2), shard(7))
+    upward = lax.rem(z + 2 + 4 * core, RING) * 2 + x
+    downward = lax.rem(z + 6 - 4 * core, RING) * 2 + x
+    pass_on(4, downward, upward)
+    pass_on("x2", shard(6), nbr)
+    pass_on("x6", shard(2), nbr)
     norm(1)
-    hand_on(2)
     unfold(1)
-    hand_on(1)
+    for k in (3, 5, 4):
+        ag_copies[k].wait_recv()
+        pass_on("x%d" % k, shard(RING - k), nbr)
     for name in ("main", "last", "tgt", "spread"):
         inputs[name].wait()
-    for copy in [swap] + passed:
-        copy.wait_recv()
-    for copy in [swap] + direct + passed:
+    for name in (1, 7, "next", "previous", "x2", "x6", "x3", "x5", "x4"):
+        ag_copies[name].wait_recv()
+    for copy in ag_copies.values():
         copy.wait_send()
 
     main = got[:, :, :WIDE].reshape(512, WIDE)
@@ -263,33 +279,42 @@
     sums = jnp.concatenate(
         [(grads[0][j] + grads[1][j]).astype(BF16) for j in range(2)], axis=0
     )
-    for block in range(4):
-        spread = jnp.dot(
-            spread_ref[block * 160 : (block + 1) * 160, :], sums, preferred_element_type=F32
-        )
-        for s in range(4):
-            part[block * 4 + s] = pack(spread[s * 40 : (s + 1) * 40])
-
-    rs = (rs_s, rs_r)
-    order = AWAY + (0,)
-    crosses = []
-    for i, k in enumerate(order):
-        copy = rcopy(part.at[ring[k] * 2 + 1 - x], x_in.at[i], rs, i, {"fsdp": nbr})
+
+    rs_copies = {}
+
+    def send(name, src, at, to):
+        copy = rcopy(src, landed.at[at], (rs_s, rs_r), at, {"fsdp": to})
         copy.start()
-        crosses.append(copy)
-    sends = []
-
-    def send_on(count):
-        for i in range(len(sends), len(sends) + count):
-            crosses[i].wait_recv()
-            stage[i] = (part[ring[AWAY[i]] * 2 + x].astype(F32) + x_in[i].astype(F32)).astype(
-                BF16
-            )
-            copy = rcopy(
-                stage.at[i], held.at[i], rs, 8 + i, {"fsdp": ring[AWAY[i]] * 2 + x}
-            )
-            copy.start()
-            sends.append(copy)
+        rs_copies[name] = (copy, at)
+
+    def arrived(name):
+        copy, at = rs_copies[name]
+        copy.wait_recv()
+        return landed[at].astype(F32)
+
+    def send_sum(name, k, column, terms, slot, at, to):
+        value = part[2 * k + column].astype(F32)
+        for term in terms:
+            value = value + term
+        stage[slot] = value.astype(BF16)
+        send(name, stage.at[slot], at, to)
+
+    for step in (4, 2, 6, 0):
+        at = pl.multiple_of((z + step) * 80, 16)
+        spread = jnp.dot(spread_ref[pl.ds(at, 160), :], sums, preferred_element_type=F32)
+        for i in range(2):
+            k = step + i
+            for c in range(2):
+                row = i * 80 + c * 40
+                part[k * 2 + c] = pack(spread[row : row + 40])
+            if 2 <= k <= 6:
+                send("x%d" % k, part.at[k * 2 + 1 - x], k, nbr)
+            elif k == 1:
+                send("side1", part.at[k * 2 + 1 - x], 7, shard(1))
+                send("own1", part.at[k * 2 + x], 8, shard(1))
+            elif k == 7:
+                send("side7", part.at[k * 2 + 1 - x], 9, shard(7))
+                send("own7", part.at[k * 2 + x], 10, shard(7))
 
     def back(i):
         products = lax.dot_general(
@@ -317,55 +342,59 @@
         results.append(result)
 
     back(0)
-    send_on(4)
+    send_sum("far4", 4, x, [arrived("x4")], 0, 11, upward)
+    send_sum("far5", 5, x, [arrived("x5")], 1, 12, shard(7))
+    send_sum("far3", 3, x, [arrived("x3")], 2, 13, shard(1))
     finish(0)
-    send_on(3)
+    send_sum("x0", 0, 1 - x, [arrived("side1"), arrived("side7")], 3, 0, nbr)
     back(1)
+    far4 = arrived("far4")
+    send_sum(
+        "own2", 2, x,
+        [arrived("x2"), arrived("far3"), jnp.where(core == 0, far4, 0.0)], 4, 14, shard(2),
+    )
+    send_sum(
+        "own6", 6, x,
+        [arrived("x6"), arrived("far5"), jnp.where(core == 1, far4, 0.0)], 5, 1, shard(6),
+    )
     finish(1)
-    crosses[7].wait_recv()
-    lane_sum = part[f].astype(F32) + x_in[7].astype(F32)
-    for i, copy in enumerate(sends):
-        copy.wait_recv()
-        lane_sum = lane_sum + held[i].astype(F32)
+    lane_sum = part[x].astype(F32)
+    for name in ("own1", "own7", "x0", "own2", "own6"):
+        lane_sum = lane_sum + arrived(name)
     lane_sum = lane_sum.astype(BF16)
-    lane_sum = jnp.concatenate([lane_sum[:, :WIDE], unpack_last(lane_sum[:, WIDE:])], axis=0)
-    row = lax.broadcasted_iota(jnp.int32, (144, BLOCK), 0)
-    col = lax.broadcasted_iota(jnp.int32, (144, BLOCK), 1)
-    expert = jnp.where(col % 12 < 6, pair_ref[0, 0], pair_ref[0, 1])
-    choose = (
-        (row // 48 == col // 12) & (row % 48 // 8 == col % 6) & (row % 8 == expert)
-    ).astype(F32).astype(BF16)
-    wide = jnp.dot(choose, lane_sum, preferred_element_type=F32).astype(BF16)
+    lane_out[...] = jnp.concatenate(
+        [lane_sum[:, :WIDE], unpack_last(lane_sum[:, WIDE:])], axis=0
+    )
+
+    dp = (dp_s, dp_r)
+    own_half = OUT_TILES // 2
+    share = own_half // chips
+    first_tile = core * own_half
+    pair = rcopy(lane_out, lane_in, dp, 30, {"dp": twin})
+    pair.start()
+    wide = jnp.dot(choose_out[...], lane_out[...], preferred_element_type=F32)
+    told.wait_recv()
+    pair.wait_recv()
+    wide = wide + jnp.dot(choose_in[...], lane_in[...], preferred_element_type=F32)
+    wide = wide.astype(BF16)
     for r in range(9):
         for t in range(TILES):
             table[r * TILES + t] = wide[r * 16 : (r + 1) * 16, t * 128 : (t + 1) * 128]
     table[OUT_TILES - 1] = jnp.zeros((16, 128), BF16)
 
-    dp = (dp_s, dp_r)
-    own_half = OUT_TILES // 2
-    share = own_half // chips
-    first_tile = core * own_half
-    pair = rcopy(
-        table.at[pl.ds(own_half - first_tile, own_half)], core_in, dp, 30, {"dp": twin}
-    )
-    pair.start()
-    pair.wait_recv()
-    half[...] = (
-        table[pl.ds(first_tile, own_half)].astype(F32) + core_in[...].astype(F32)
-    ).astype(BF16)
     scatters = []
     for i, peer in enumerate(peers):
         copy = rcopy(
-            half.at[pl.ds(peer * share, share)], chunk_in.at[i], dp, i,
+            table.at[pl.ds(first_tile + peer * share, share)], chunk_in.at[i], dp, i,
             {"dp": peer * 2 + core},
         )
         copy.start()
         scatters.append(copy)
-    acc = half[pl.ds(chip * share, share)].astype(F32)
+    own = pl.ds(first_tile + chip * share, share)
+    acc = table[own].astype(F32)
     for i, copy in enumerate(scatters):
         copy.wait_recv()
         acc = acc + chunk_in[i].astype(F32)
-    own = pl.ds(first_tile + chip * share, share)
     full[own] = acc.astype(BF16)
     gathers = []
     for i, peer in enumerate(peers):
@@ -378,6 +407,18 @@
     last = rcopy(full.at[mine], full.at[mine], dp, 31, {"dp": twin})
     last.start()
     last.wait_recv()
+    for copy in results:
+        copy.wait()
+    for copy in [copy for copy, _ in rs_copies.values()] + [pair, told, last] + scatters + gathers:
+        copy.wait_send()
+
+
+def finish_kernel(full, gi_in, gw_ref, gi_out, gi_ref, sem):
+    move = pltpu.make_async_copy(gi_in, gi_ref, sem.at[0])
+    move.start()
+    move.wait()
+    move = pltpu.make_async_copy(gi_ref, gi_out, sem.at[1])
+    move.start()
     for dx in range(3):
         for r in range(6):
             at = dx * 6 + r
@@ -386,10 +427,7 @@
                 axis=1,
             )
             gw_ref[r, :, dx * SPAN : (dx + 1) * SPAN] = line[:, :SPAN]
-    for copy in results:
-        copy.wait()
-    for copy in crosses + sends + [pair, last] + scatters + gathers:
-        copy.wait_send()
+    move.wait()
 
 
 def local(
@@ -410,10 +448,10 @@
     smem = pl.BlockSpec(memory_space=pltpu.SMEM)
     sems = pltpu.SemaphoreType.DMA
     hbm = pl.BlockSpec(memory_space=pltpu.MemorySpace.HBM)
-    grad_weight, grad_input = pl.pallas_call(
+    full, grad_input = pl.pallas_call(
         functools.partial(kernel, chips),
         out_shape=(
-            jax.ShapeDtypeStruct((6, 8, 3 * SPAN), F32),
+            jax.ShapeDtypeStruct((OUT_TILES, 16, 128), BF16),
             jax.ShapeDtypeStruct((2, C, CELLS), BF16),
         ),
         in_specs=[hbm, hbm, smem, smem, hbm, vmem, vmem, hbm, smem, smem] + [hbm] * 4,
@@ -438,20 +476,20 @@
             pltpu.VMEM((2, 288, CELLS), BF16),
             pltpu.VMEM((C, CELLS), F32),
             pltpu.VMEM((16,) + PACK, BF16),
-            pltpu.VMEM((8,) + PACK, BF16),
-            pltpu.VMEM((7,) + PACK, BF16),
-            pltpu.VMEM((7,) + PACK, BF16),
+            pltpu.VMEM((15,) + PACK, BF16),
+            pltpu.VMEM((6,) + PACK, BF16),
+            pltpu.VMEM((144, BLOCK), BF16),
+            pltpu.VMEM((144, BLOCK), BF16),
+            pltpu.VMEM((BLOCK, WIDE), BF16),
+            pltpu.VMEM((BLOCK, WIDE), BF16),
             pltpu.VMEM((OUT_TILES, 16, 128), BF16),
-            pltpu.VMEM((OUT_TILES // 2, 16, 128), BF16),
-            pltpu.VMEM((OUT_TILES // 2, 16, 128), BF16),
             pltpu.VMEM((15, OUT_TILES // 2 // chips, 16, 128), BF16),
-            pltpu.VMEM((OUT_TILES, 16, 128), BF16),
             sems((15,)),
             sems((15,)),
             sems((15,)),
             sems((15,)),
-            sems((32,)),
-            sems((32,)),
+            sems((33,)),
+            sems((33,)),
             sems((10,)),
         ],
         compiler_params=pltpu.CompilerParams(
@@ -464,6 +502,16 @@
         jnp.asarray(main, BF16), jnp.asarray(last, BF16), jnp.asarray(spread, BF16),
         jnp.asarray(group, F32),
     )
+    grad_weight, grad_input = pl.pallas_call(
+        finish_kernel,
+        out_shape=(
+            jax.ShapeDtypeStruct((6, 8, 3 * SPAN), F32),
+            jax.ShapeDtypeStruct((2, C, CELLS), BF16),
+        ),
+        in_specs=[vmem, hbm],
+        out_specs=(vmem, hbm),
+        scratch_shapes=[pltpu.VMEM((2, C, CELLS), BF16), sems((2,))],
+    )(full, grad_input)
     return grad_weight.swapaxes(0, 1), grad_input
 
 

time: 76.1 us -> 73.4 us (0.965)
  local copies, waits for them, and re-layouts: 2.66 us -> 0 us
    pallas_call x0 -> x1, Pallas kernels: none -> 3.49 us  [local(): pl.pallas_call(finish_kernel, out_shape=(jax.ShapeDtypeStruct((6, 8, 3 *...]
    pallas_call x1, Pallas kernels: 72.6 us -> 69.1 us  [local(): pl.pallas_call(functools.partial(kernel, chips), out_shape=(jax.ShapeDtyp...]
    unnamed x4 -> x0, local copies, waits for them, and re-layouts: 2.66 us -> none
where the time goes in v4:
time: 73.4 us; the launch traced here: 73.2 us
  Pallas kernels  72.6 us (99%)
    pallas_call x1, Pallas kernels, local(): pl.pallas_call(functools.partial(kernel, chips), out_shape=(jax.ShapeDtyp...  69.1 us
    pallas_call x1, Pallas kernels, local(): pl.pallas_call(finish_kernel, out_shape=(jax.ShapeDtypeStruct((6, 8, 3 *...  3.49 us

profile of v4, /device:TPU:1, one launch (start us, length us, event | category | flops | bytes accessed | tf_op | source)
XLA Modules:
  0.0 73.2 jit_solution(576577043675238868)
XLA Ops:
  0.6 69.1 %shard_map.149 = (bf16[64,16,128]{2,1,0:T(8,128)(2,1)}, bf16[2,96,1024]{2,1,0:T(8,128)(2,1)}) custom-call(bf16[2,96,1024]{2,1,0:T(8,128)(2,1)} %lat_hbm.1, bf16[2,96,1024]{2,1,0:T(8,128)(2,1)} %tgt_hbm.1, f32[2]{0:T(128)} %reward_ref.1, s32[2]{0:T(128)} %step_ref.1, f32[96,1000]{1,0:T(8,128)} %bitcast.7, f32[1,96]{1,0:T(1,128)} %bitcast.9, ...), custom_call_target="tpu_custom_call" | custom-call | tf_op jit(solution)/shard_map/pallas_call | solution.py:451
  69.7 3.5 %shard_map.150 = (f32[6,8,2592]{2,1,0:T(8,128)}, bf16[2,96,1024]{2,1,0:T(8,128)(2,1)}) custom-call(bf16[64,16,128]{2,1,0:T(8,128)(2,1)} %get-tuple-element.6.full, bf16[2,96,1024]{2,1,0:T(8,128)(2,1)} %get-tuple-element.7.gi_in), custom_call_target="tpu_custom_call" | custom-call | tf_op jit(solution)/shard_map/pallas_call | solution.py:505

commit v5 on v4

--- a/solution.py
+++ b/solution.py
@@ -95,10 +95,10 @@
 
 def kernel(
     chips,
-    lat_hbm, tgt_hbm, reward_ref, step_ref, time_hbm, gain_ref, bias_ref, weight_hbm, pair_ref,
-    count_ref, main_hbm, last_hbm, spread_hbm, group_hbm,
+    lat_hbm, tgt_hbm, reward_hbm, step_hbm, time_hbm, gain_hbm, bias_hbm, weight_hbm, pair_hbm,
+    count_hbm, main_hbm, last_hbm, spread_hbm, group_hbm,
     full, gi_hbm,
-    gi_ref, weight_ref, lat_ref, tgt_ref, time_ref, main_ref, last_ref, spread_ref, group_ref,
+    reward_ref, step_ref, gain_ref, bias_ref, pair_ref, count_ref, gi_ref, weight_ref, lat_ref, tgt_ref, time_ref, main_ref, last_ref, spread_ref, group_ref,
     got, normed, slope, rstd, cols, both, ups, ucat, fold, part, landed, stage,
     choose_out, choose_in, lane_out, lane_in, table, chunk_in,
     ag_s, ag_r, rs_s, rs_r, dp_s, dp_r, in_s,
@@ -123,7 +123,9 @@
         )
     inputs = {}
     for at, (name, src, dst) in enumerate((
-        ("weight", weight_hbm, weight_ref), ("lat", lat_hbm, lat_ref),
+        ("pair", pair_hbm, pair_ref), ("weight", weight_hbm, weight_ref),
+        ("step", step_hbm, step_ref), ("gain", gain_hbm, gain_ref), ("bias", bias_hbm, bias_ref),
+        ("count", count_hbm, count_ref), ("reward", reward_hbm, reward_ref), ("lat", lat_hbm, lat_ref),
         ("time", time_hbm, time_ref), ("group", group_hbm, group_ref),
         ("main", main_hbm, main_ref), ("last", last_hbm, last_ref), ("tgt", tgt_hbm, tgt_ref),
         ("spread", spread_hbm, spread_ref),
@@ -131,6 +133,7 @@
         inputs[name] = pltpu.make_async_copy(src, dst, in_s.at[at])
         inputs[name].start()
 
+    inputs["pair"].wait()
     row = lax.broadcasted_iota(jnp.int32, (16, 48), 0)
     col = lax.broadcasted_iota(jnp.int32, (16, 48), 1)
     expert = jnp.where(row < 6, pair_ref[0, 0], pair_ref[0, 1] - 48)
@@ -171,6 +174,8 @@
     eye = (
         lax.broadcasted_iota(jnp.int32, (C, C), 0) == lax.broadcasted_iota(jnp.int32, (C, C), 1)
     ).astype(F32)
+    for name in ("step", "gain", "bias", "count", "reward"):
+        inputs[name].wait()
     gain = column_of(gain_ref[...], eye)
     bias = column_of(bias_ref[...], eye)
     lane = lax.broadcasted_iota(jnp.int32, (C, CELLS), 1)
@@ -337,7 +342,7 @@
         flow = fold[...] * slope[i]
         start = rstd[i][:, :1] * (flow - group_mean(flow) - value * group_mean(flow * value))
         gi_ref[i] = (ups[i] + start).astype(BF16)
-        result = pltpu.make_async_copy(gi_ref.at[i], gi_hbm.at[i], in_s.at[8 + i])
+        result = pltpu.make_async_copy(gi_ref.at[i], gi_hbm.at[i], in_s.at[14 + i])
         result.start()
         results.append(result)
 
@@ -413,21 +418,30 @@
         copy.wait_send()
 
 
-def finish_kernel(full, gi_in, gw_ref, gi_out, gi_ref, sem):
-    move = pltpu.make_async_copy(gi_in, gi_ref, sem.at[0])
-    move.start()
-    move.wait()
-    move = pltpu.make_async_copy(gi_ref, gi_out, sem.at[1])
-    move.start()
-    for dx in range(3):
-        for r in range(6):
+def finish_kernel(full_hbm, gi_in, gw_hbm, gi_out, full, gi_ref, gw_ref, sem):
+    moves = [
+        pltpu.make_async_copy(full_hbm, full, sem.at[0]),
+        pltpu.make_async_copy(gi_in, gi_ref, sem.at[1]),
+    ]
+    for move in moves:
+        move.start()
+    for move in moves:
+        move.wait()
+    moves = [pltpu.make_async_copy(gi_ref, gi_out, sem.at[2])]
+    moves[0].start()
+    for r in range(6):
+        for dx in range(3):
             at = dx * 6 + r
             line = jnp.concatenate(
                 [full[at // 2 * TILES + t].astype(F32)[at % 2 * 8 :][:8] for t in range(TILES)],
                 axis=1,
             )
             gw_ref[r, :, dx * SPAN : (dx + 1) * SPAN] = line[:, :SPAN]
-    move.wait()
+        move = pltpu.make_async_copy(gw_ref.at[r], gw_hbm.at[r], sem.at[3 + r])
+        move.start()
+        moves.append(move)
+    for move in moves:
+        move.wait()
 
 
 def local(
@@ -445,7 +459,7 @@
 ):
     main, last, spread, group = constants()
     vmem = pl.BlockSpec(memory_space=pltpu.VMEM)
-    smem = pl.BlockSpec(memory_space=pltpu.SMEM)
+    smem = pltpu.MemorySpace.SMEM
     sems = pltpu.SemaphoreType.DMA
     hbm = pl.BlockSpec(memory_space=pltpu.MemorySpace.HBM)
     full, grad_input = pl.pallas_call(
@@ -454,9 +468,15 @@
             jax.ShapeDtypeStruct((OUT_TILES, 16, 128), BF16),
             jax.ShapeDtypeStruct((2, C, CELLS), BF16),
         ),
-        in_specs=[hbm, hbm, smem, smem, hbm, vmem, vmem, hbm, smem, smem] + [hbm] * 4,
+        in_specs=[hbm] * 14,
         out_specs=(vmem, hbm),
         scratch_shapes=[
+            smem((2,), F32),
+            smem((2,), jnp.int32),
+            pltpu.VMEM((1, C), F32),
+            pltpu.VMEM((1, C), F32),
+            smem((1, 2), jnp.int32),
+            smem((1, 2), jnp.int32),
             pltpu.VMEM((2, C, CELLS), BF16),
             pltpu.VMEM((48, 3 * SPAN), BF16),
             pltpu.VMEM((2, C, CELLS), BF16),
@@ -490,7 +510,7 @@
             sems((15,)),
             sems((33,)),
             sems((33,)),
-            sems((10,)),
+            sems((16,)),
         ],
         compiler_params=pltpu.CompilerParams(
             collective_id=0, has_side_effects=True, vmem_limit_bytes=60 * 2**20
@@ -508,9 +528,14 @@
             jax.ShapeDtypeStruct((6, 8, 3 * SPAN), F32),
             jax.ShapeDtypeStruct((2, C, CELLS), BF16),
         ),
-        in_specs=[vmem, hbm],
-        out_specs=(vmem, hbm),
-        scratch_shapes=[pltpu.VMEM((2, C, CELLS), BF16), sems((2,))],
+        in_specs=[hbm, hbm],
+        out_specs=(hbm, hbm),
+        scratch_shapes=[
+            pltpu.VMEM((OUT_TILES, 16, 128), BF16),
+            pltpu.VMEM((2, C, CELLS), BF16),
+            pltpu.VMEM((6, 8, 3 * SPAN), F32),
+            sems((9,)),
+        ],
     )(full, grad_input)
     return grad_weight.swapaxes(0, 1), grad_input
 

time: 73.4 us -> 71.3 us (0.971)
  Pallas kernels: 72.6 us -> 70.5 us
    pallas_call x1, Pallas kernels: 3.49 us -> 2.06 us  [local(): pl.pallas_call(finish_kernel, out_shape=(jax.ShapeDtypeStruct((6, 8, 3 *...]
where the time goes in v5:
time: 71.3 us; the launch traced here: 71.2 us
  Pallas kernels  70.5 us (99%)
    pallas_call x1, Pallas kernels, local(): pl.pallas_call(functools.partial(kernel, chips), out_shape=(jax.ShapeDtyp...  68.5 us
    pallas_call x1, Pallas kernels, local(): pl.pallas_call(finish_kernel, out_shape=(jax.ShapeDtypeStruct((6, 8, 3 *...  2.06 us

profile of v5, /device:TPU:1, one launch (start us, length us, event | category | flops | bytes accessed | tf_op | source)
XLA Modules:
  0.0 71.2 jit_solution(17807024995024320276)
XLA Ops:
  0.6 68.5 %shard_map.149 = (bf16[64,16,128]{2,1,0:T(8,128)(2,1)}, bf16[2,96,1024]{2,1,0:T(8,128)(2,1)}) custom-call(bf16[2,96,1024]{2,1,0:T(8,128)(2,1)} %lat_hbm.1, bf16[2,96,1024]{2,1,0:T(8,128)(2,1)} %tgt_hbm.1, f32[2]{0:T(128)} %reward_hbm.1, s32[2]{0:T(128)} %step_hbm.1, f32[96,1000]{1,0:T(8,128)} %bitcast.7, f32[1,96]{1,0:T(1,128)} %bitcast.9, ...), custom_call_target="tpu_custom_call" | custom-call | tf_op jit(solution)/shard_map/pallas_call | solution.py:465
  69.1 2.1 %shard_map.150 = (f32[6,8,2592]{2,1,0:T(8,128)}, bf16[2,96,1024]{2,1,0:T(8,128)(2,1)}) custom-call(bf16[64,16,128]{2,1,0:T(8,128)(2,1)} %get-tuple-element.6.full_hbm, bf16[2,96,1024]{2,1,0:T(8,128)(2,1)} %get-tuple-element.7.gi_in), custom_call_target="tpu_custom_call" | custom-call | tf_op jit(solution)/shard_map/pallas_call | solution.py:525

commit v6 on v5

--- a/solution.py
+++ b/solution.py
@@ -111,7 +111,8 @@
     core = d % 2
     chip = d // 2
     twin = chip * 2 + 1 - core
-    peers = [lax.rem(chip + i, chips) for i in range(1, chips)]
+    farthest = sorted(range(1, chips), key=lambda i: -min(i % 8, 8 - i % 8))
+    peers = [lax.rem(chip + i, chips) for i in farthest]
     ring = {k: lax.rem(z + k, RING) for k in range(RING)}
     barrier = pltpu.get_barrier_semaphore()
     for other in [nbr] + [ring[k] * 2 + x for k in (1, 7, 2, 6)]:
@@ -147,27 +148,26 @@
     got[f] = pack(stacked)
     pl.semaphore_wait(barrier, 6 + len(peers))
 
+    ag_copies = {}
+
+    def pass_on(name, item, to):
+        at = len(ag_copies)
+        copy = rcopy(got.at[item], got.at[item], (ag_s, ag_r), at, {"fsdp": to})
+        copy.start()
+        ag_copies[name] = copy
+
+    def shard(k):
+        return ring[k] * 2 + x
+
+    pass_on("swap", f, nbr)
+    for k in (2, 6, 1, 7):
+        pass_on(k, f, shard(k))
     row = lax.broadcasted_iota(jnp.int32, (144, BLOCK), 0)
     col = lax.broadcasted_iota(jnp.int32, (144, BLOCK), 1)
     expert = jnp.where(col % 12 < 6, pair_ref[0, 0], pair_ref[0, 1])
     choose_out[...] = (
         (row // 48 == col // 12) & (row % 48 // 8 == col % 6) & (row % 8 == expert)
     ).astype(F32).astype(BF16)
-
-    ag_copies = {}
-
-    def pass_on(name, item, to):
-        at = len(ag_copies)
-        copy = rcopy(got.at[item], got.at[item], (ag_s, ag_r), at, {"fsdp": to})
-        copy.start()
-        ag_copies[name] = copy
-
-    def shard(k):
-        return ring[k] * 2 + x
-
-    pass_on("swap", f, nbr)
-    for k in (2, 6, 1, 7):
-        pass_on(k, f, shard(k))
     told = rcopy(choose_out, choose_in, (dp_s, dp_r), 32, {"dp": twin})
     told.start()
 

time: 71.3 us -> 71.2 us (level)
  no operation moved by 1% of the time
where the time goes in v6:
time: 71.2 us; the launch traced here: 71.1 us
  Pallas kernels  70.5 us (99%)
    pallas_call x1, Pallas kernels, local(): pl.pallas_call(functools.partial(kernel, chips), out_shape=(jax.ShapeDtyp...  68.4 us
    pallas_call x1, Pallas kernels, local(): pl.pallas_call(finish_kernel, out_shape=(jax.ShapeDtypeStruct((6, 8, 3 *...  2.06 us

profile of v6, /device:TPU:1, one launch (start us, length us, event | category | flops | bytes accessed | tf_op | source)
XLA Modules:
  0.0 71.1 jit_solution(13428021726822465856)
XLA Ops:
  0.6 68.4 %shard_map.149 = (bf16[64,16,128]{2,1,0:T(8,128)(2,1)}, bf16[2,96,1024]{2,1,0:T(8,128)(2,1)}) custom-call(bf16[2,96,1024]{2,1,0:T(8,128)(2,1)} %lat_hbm.1, bf16[2,96,1024]{2,1,0:T(8,128)(2,1)} %tgt_hbm.1, f32[2]{0:T(128)} %reward_hbm.1, s32[2]{0:T(128)} %step_hbm.1, f32[96,1000]{1,0:T(8,128)} %bitcast.7, f32[1,96]{1,0:T(1,128)} %bitcast.9, ...), custom_call_target="tpu_custom_call" | custom-call | tf_op jit(solution)/shard_map/pallas_call | solution.py:465
  69.1 2.1 %shard_map.150 = (f32[6,8,2592]{2,1,0:T(8,128)}, bf16[2,96,1024]{2,1,0:T(8,128)(2,1)}) custom-call(bf16[64,16,128]{2,1,0:T(8,128)(2,1)} %get-tuple-element.6.full_hbm, bf16[2,96,1024]{2,1,0:T(8,128)(2,1)} %get-tuple-element.7.gi_in), custom_call_target="tpu_custom_call" | custom-call | tf_op jit(solution)/shard_map/pallas_call | solution.py:525
